TPU v7x, 256 devices: a whole 4x4x8 slice. The times are simulated.
256 devices in a mesh: pts: 16 (over z, core), hrs: 8 (over y_hi, x), bins: 2 (over y_lo).
Axes of the slice: x: 4, y: 4 (y_hi: 2, y_lo: 2; y = y_hi * 2 + y_lo), z: 8, core: 2. Of those that a mesh axis runs over, the one named last changes fastest.
Arguments:
- tensor: float32 [128, 4096, 1296], P('hrs', 'pts', 'bins'), may hold values from -6 to 6
- b_factor: float32 [4096, 256], P(('pts', 'hrs')), as said below
- c_factor: float32 [1296, 256], P('bins'), as said below
Outputs:
- hour_factor: float32 [128, 256], P('hrs')
- point_factor: float32 [4096, 256], P(('pts', 'hrs'))
Inputs may be any that keep to these rules, and one draw needn't show every extreme that they name: `b_factor`: real-valued factor rows. `c_factor`: real-valued factor rows.
All inputs are finite; a program needn't handle non-finite values.
Results may differ from a plain program's by a relative error of at most 0.00018.
Values sent between devices are 32-bit elements; how exact they have to be, the bound alone decides.
A program may use at most 64 MiB of HBM per device.

v0:
```python
import jax
import jax.numpy as jnp
from jax import lax
from jax.sharding import PartitionSpec as P


def normal_solve(rhs, hadamard):
    factor = jnp.linalg.cholesky(hadamard)
    return jax.scipy.linalg.cho_solve((factor, True), rhs.T).T


def local(tensor, b_factor, c_factor):
    highest = lax.Precision.HIGHEST
    hour_rows, point_rows, bin_rows = tensor.shape
    width = c_factor.shape[1]
    gram_c = lax.psum(jnp.dot(c_factor.T, c_factor, precision=highest), "bins")
    b_block = lax.all_gather(b_factor, "hrs", axis=0, tiled=True)
    gram_b = lax.psum(jnp.dot(b_factor.T, b_factor, precision=highest), ("pts", "hrs"))
    contracted = jnp.dot(
        tensor.reshape(hour_rows * point_rows, bin_rows), c_factor, precision=highest
    )
    contracted = contracted.reshape(hour_rows, point_rows, width)
    mttkrp_hours = jnp.einsum("ijr,jr->ir", contracted, b_block, precision=highest)
    mttkrp_hours = lax.psum(mttkrp_hours, ("pts", "bins"))
    hour_factor = normal_solve(mttkrp_hours, gram_b * gram_c)
    gram_a = lax.psum(jnp.dot(hour_factor.T, hour_factor, precision=highest), "hrs")
    hadamard = gram_a * gram_c
    mttkrp_points = jnp.einsum("ijr,ir->jr", contracted, hour_factor, precision=highest)
    owned = lax.psum_scatter(mttkrp_points, "hrs", scatter_dimension=0, tiled=True)
    owned = lax.psum(owned, "bins")
    point_factor = normal_solve(owned, hadamard)
    return (hour_factor, point_factor)


def solution(mesh):
    placed = (P("hrs", "pts", "bins"), P(("pts", "hrs"), None), P("bins", None))
    return jax.shard_map(
        local,
        mesh=mesh,
        in_specs=placed,
        out_specs=(P("hrs", None), P(("pts", "hrs"), None)),
        check_vma=False,
    )
```

profile of v0, /device:TPU:8, one launch (start us, length us, event | category | flops | bytes accessed | tf_op | source)
XLA Modules:
  0.0 1435.6 jit_solution(10058796177812686441)
XLA Ops:
  7.2 0.0 all-reduce.7.cloned.1.call-start
  7.2 1.0 copy-done
  8.3 2.2 fusion.29
  10.4 0.0 all-reduce.7.cloned.1.call-update
  10.4 0.0 all-reduce.5.cloned.1.call-start
  10.5 2.0 fusion.28
  12.5 0.0 all-reduce.5.cloned.1.call-update
  12.5 0.0 all-reduce.9.cloned.1.call-start
  12.5 34.8 %all_gather.3 = f32[256,256]{1,0:T(8,128)S(1)} all-gather(f32[32,256]{1,0:T(8,128)} %param.5), channel_id=1, replica_groups=mesh['pts'=16,'hrs'=8,'bins'=2] {'hrs'}, dimensions={0}, use_global_device_ids=true | all-gather | bytes 294912 | tf_op jit(solution)/shard_map/all_gather | solution.py:17
  47.4 24.0 %multiply_reduce_fusion.1 = (f32[256,16]{0,1:T(8,128)S(1)}, f32[16,256,256]{2,1,0:T(8,128)}) fusion(f32[256,256]{0,1:T(8,128)S(1)} %bitcast.97, f32[16,256,648]{1,2,0:T(8,128)} %param.4, f32[648,256]{1,0:T(8,128)S(1)} %copy-done), kind=kOutput, calls=%fused_computation.5 | convolution fusion | flops 8155820032 | bytes 15753216 | tf_op jit(solution)/shard_map/dot_general | solution.py:19
  71.3 0.1 copy.23
  71.4 108.9 %psum.37 = f32[256,16]{1,0:T(8,128)S(1)} all-reduce(f32[256,16]{1,0:T(8,128)S(1)} %copy.23), channel_id=1, replica_groups=mesh['pts'=16,'hrs'=8,'bins'=2] {'pts','bins'}, use_global_device_ids=true, to_apply=%region_6.8 | all-reduce | flops 4096 | bytes 32768 | tf_op jit(solution)/shard_map/psum | solution.py:24
  180.3 1008.3 %all-reduce.5.cloned.1.call-done = f32[256,256]{0,1:T(8,128)} async-done(((f32[256,256]{0,1:T(8,128)}), f32[256,256]{0,1:T(8,128)}) %all-reduce.5.cloned.1.call-update) | async-done | bytes 262160 | tf_op jit(solution)/shard_map/psum | solution.py:18
  1188.7 1.1 mul.6
  1189.7 0.1 copy.12
  1189.9 11.7 cholesky.130
  1201.7 9.8 custom-call.25
  1211.5 0.2 constant_dynamic-update-slice_fusion.3
  1211.7 0.3 convolution_subtract_fusion.3
  1212.0 11.7 cholesky.147
  1223.8 0.7 compare_reduce_fusion.2
  1225.8 0.1 triangular_solve.114
  1225.9 4.0 while.2
  1225.9 0.6 fusion.51
  1226.5 1.4 bitcast_dynamic-update-slice_fusion.4
  1227.9 0.6 fusion.51
  1228.5 1.4 bitcast_dynamic-update-slice_fusion.4
  1229.8 19.7 %custom-call.22 = f32[2,128,128]{1,2,0:T(8,128)S(1)} custom-call(f32[2,128,128]{2,1,0:T(8,128)S(1)} %get-tuple-element.10), custom_call_target="InvertDiagBlocksLowerTriangular" | custom-call | tf_op jit(solution)/shard_map/jit(_cho_solve)/triangular_solve | solution.py:9
  1249.5 0.2 fusion.8
  1249.7 0.2 convolution_subtract_fusion.2
  1250.0 0.3 fusion.16
  1250.3 0.2 fusion.15
  1250.5 0.2 convolution_subtract_fusion.5
  1250.7 0.2 fusion.14
  1250.9 1.2 fusion.24
  1252.1 0.6 pad_maximum_fusion
  1252.7 0.2 reduce-scatter.4.cloned.1.call-start
  1252.9 3.2 multiply_reduce_fusion
  1256.2 82.4 %all-reduce.9.cloned.1.call-done = f32[256,256]{0,1:T(8,128)} async-done(((f32[256,256]{0,1:T(8,128)}), f32[256,256]{0,1:T(8,128)}) %all-reduce.9.cloned.1.call-update) | async-done | bytes 262160 | tf_op jit(solution)/shard_map/psum | solution.py:26
  1338.7 1.0 mul.7
  1339.7 0.1 copy.14
  1339.9 11.7 cholesky.164
  1351.6 9.8 custom-call.26
  1361.4 0.2 constant_dynamic-update-slice_fusion.1
  1361.6 0.3 convolution_subtract_fusion.1
  1361.9 11.7 cholesky.181
  1373.7 0.7 compare_reduce_fusion
  1374.4 0.7 compare_reduce_fusion.1
  1376.4 4.2 while.3
  1376.6 0.6 fusion.52
  1377.2 1.4 bitcast_dynamic-update-slice_fusion.5
  1378.6 0.6 fusion.52
  1379.2 1.4 bitcast_dynamic-update-slice_fusion.5
  1380.6 19.7 %custom-call.23 = f32[2,128,128]{1,2,0:T(8,128)S(1)} custom-call(f32[2,128,128]{2,1,0:T(8,128)S(1)} %get-tuple-element.18), custom_call_target="InvertDiagBlocksLowerTriangular" | custom-call | tf_op jit(solution)/shard_map/jit(_cho_solve)/triangular_solve | solution.py:9
  1400.3 16.4 %reduce-scatter.4.cloned.1.call-done = f32[32,256]{1,0:T(8,128)} async-done(((f32[256,256]{1,0:T(8,128)}), f32[32,256]{1,0:T(8,128)}) %reduce-scatter.4.cloned.1.call-update) | async-done | bytes 32784
  1416.7 0.9 copy.33
  1417.5 9.3 psum.39
  1426.8 0.3 fusion.4
  1427.1 0.2 convolution_subtract_fusion
  1427.3 0.3 fusion.19
  1427.6 0.2 fusion.18
  1427.8 0.2 convolution_subtract_fusion.4
  1428.0 0.2 fusion.17
  1428.2 0.6 maximum_bitcast_fusion
  (25 shorter events, 0.4 us)
Async XLA Ops:
  7.2 1.1 copy-start
  7.2 173.2 %all-reduce.7.cloned.1.call-start = ((), (), s32[]{:S(2)}) async-start(), calls=%async_computation.2 | async-start | bytes 524288 | tf_op jit(solution)/shard_map/psum | solution.py:16
  10.4 1178.2 %all-reduce.5.cloned.1.call-start = ((), (), s32[]{:S(2)}) async-start(), calls=%async_computation.1 | async-start | bytes 524288 | tf_op jit(solution)/shard_map/psum | solution.py:18
  12.5 1326.2 %all-reduce.9.cloned.1.call-start = ((), (), s32[]{:S(2)}) async-start(), calls=%async_computation.3 | async-start | bytes 524288 | tf_op jit(solution)/shard_map/psum | solution.py:26
  1211.5 127.1 %copy-start.1 = (f32[256,256]{0,1:T(8,128)S(1)}, f32[256,256]{0,1:T(8,128)}, u32[]{:S(2)}) copy-start(f32[256,256]{0,1:T(8,128)} %all-reduce.7.cloned.1.call-done) | copy-start | bytes 786436
  1252.7 164.0 %reduce-scatter.4.cloned.1.call-start = ((), (), s32[]{:S(2)}) async-start(), calls=%async_computation.4 | async-start | bytes 294912
Sparse Core Ops, SparseCore 0:
  10.6 37.2 all-reduce.6
  50.7 1137.9 all-reduce.4
  1252.8 85.7 all-reduce.8
  1342.9 73.7 reduce-scatter.3
where the time goes:
time: 1450 us; the launch traced here: 1440 us
  waiting for transfers between devices  1110 us (77%)
  blocking collectives  153 us (11%)
  other arithmetic  115 us (8%)
  matrix products  32.9 us (2%)
  between operations  16.8 us (1%)
    psum x1, waiting for transfers between devices, local(): lax.psum(jnp.dot(b_factor.T, b_factor, precision=highest), ('pts', 'hrs'))  1010 us
    psum x1, blocking collectives, local(): mttkrp_hours = lax.psum(mttkrp_hours, ('pts', 'bins'))  109 us
    psum x1, waiting for transfers between devices, local(): lax.psum(jnp.dot(hour_factor.T, hour_factor, precision=highest), 'hrs')  82.4 us
    another operation x13, other arithmetic, normal_solve(): factor = jnp.linalg.cholesky(hadamard)  68.7 us
    another operation x6, other arithmetic, normal_solve(): return jax.scipy.linalg.cho_solve((factor, True), rhs.T).T  40 us
    all_gather x1, blocking collectives, local(): b_block = lax.all_gather(b_factor, 'hrs', axis=0, tiled=True)  34.8 us
  transfers between devices with their start and end apart: 4, of which 3 were waited for; matrix products, arithmetic and copies ran while one was open for 6% of the time, Pallas kernels for 0%

commit v1 on v0

v1 whole, which is shorter than its diff:
```python
import functools

import jax
import jax.numpy as jnp
from jax import lax
from jax.experimental import pallas as pl
from jax.experimental.pallas import tpu as pltpu
from jax.sharding import PartitionSpec as P

f32 = jnp.float32
bf16 = jnp.bfloat16
HIGHEST = lax.Precision.HIGHEST
MESH = pl.DeviceIdType.MESH
CONTRACT_ROWS = (((0,), (0,)), ((), ()))


def gram(x):
    return lax.dot_general(
        x, x, CONTRACT_ROWS, precision=HIGHEST, preferred_element_type=f32
    )


def split(x):
    first = x.astype(bf16).astype(f32)
    rest = x - first
    second = rest.astype(bf16).astype(f32)
    return first, second, rest - second


def reciprocal(x):
    y = pltpu.reciprocal(x, approx=True)
    y = y * (2.0 - x * y)
    return y * (2.0 - x * y)


def eliminate(k, a):
    width = a.shape[1]
    row = pl.multiple_of(k * 8, 8)
    panel = a[pl.ds(row, 8), :]
    tile = pl.multiple_of((k // 16) * 128, 128)
    pivots = pltpu.roll(
        a[pl.ds(row, 8), pl.ds(tile, 128)], lax.rem(128 - lax.rem(k, 16) * 8, 128), 1
    )
    lane = lax.broadcasted_iota(jnp.int32, (8, width), 1)
    sub = lax.broadcasted_iota(jnp.int32, (8, width), 0)
    sub1 = lax.broadcasted_iota(jnp.int32, (8, 128), 0)
    rel = lane - row
    inside = (rel >= 0) & (rel < 8)
    column = jnp.where(lane < row, -panel, panel)
    work = jnp.where(inside, jnp.where(rel == sub, 1.0, 0.0), panel)
    cols = [jnp.broadcast_to(pivots[:, j : j + 1], (8, 128)) for j in range(8)]
    data = [work[:, s : s + 128] for s in range(0, width, 128)]
    for j in range(8):
        state = cols[j:] + data
        rows = [jnp.broadcast_to(x[j : j + 1, :], (8, 128)) for x in state]
        inverse = reciprocal(rows[0])
        factor = jnp.where(sub1 == j, 1.0 - inverse, cols[j] * inverse)
        state = [x - factor * r for x, r in zip(state, rows)]
        cols = cols[:j] + state[: 8 - j]
        data = state[8 - j :]
    panel = jnp.concatenate(data, axis=1)
    c1, c2, c3 = split(column)
    r1, r2, r3 = split(panel)
    left = jnp.concatenate([c1, c1, c2, c2, c1, c3], axis=0).astype(bf16)
    right = jnp.concatenate([r1, r2, r1, r2, r3, r1], axis=0).astype(bf16)
    update = lax.dot_general(
        left, right, CONTRACT_ROWS, preferred_element_type=f32
    )
    rel = lax.broadcasted_iota(jnp.int32, a.shape, 1) - row
    a[...] = jnp.where((rel >= 0) & (rel < 8), 0.0, a[...]) - update
    a[pl.ds(row, 8), :] = panel


def kernel(
    sizes,
    t_hbm,
    b_hbm,
    c_hbm,
    hf_ref,
    pf_ref,
    tbuf,
    con,
    cbuf,
    chi,
    clo,
    bbuf,
    gb_part,
    gc_part,
    gb_in,
    gc_in,
    gb_z,
    hmat,
    gcm,
    mh,
    mh_core,
    mh_mine,
    mh_bins,
    mh_z,
    mh_all,
    hfall,
    mp,
    mp_in,
    owned,
    lsem,
    ssem,
    rsem,
):
    NP, NH, NB = sizes
    Z, Q = NP // 2, NH * NB
    hours, points, _ = t_hbm.shape
    width = c_hbm.shape[1]
    half = width // 2
    prow = half // Q
    brow = b_hbm.shape[0]
    mrow = points // Q
    hh = hours // 2
    p, h, n = lax.axis_index("pts"), lax.axis_index("hrs"), lax.axis_index("bins")
    z, core = p // 2, lax.rem(p, 2)
    q = h * NB + n

    def plane(d):
        t = lax.rem(q + d, Q)
        return (p, t // NB, lax.rem(t, NB))

    def along_hours(d):
        return (p, lax.rem(h + d, NH), n)

    def along_z(d):
        return (lax.rem(z + d, Z) * 2 + core, h, n)

    other_core = (p + 1 - 2 * core, h, n)
    other_bins = (p, h, 1 - n)

    def remote(src, dst, i, target):
        return pltpu.make_async_remote_copy(
            src_ref=src,
            dst_ref=dst,
            send_sem=ssem.at[i],
            recv_sem=rsem.at[i],
            device_id=target,
            device_id_type=MESH,
        )

    def start_all(count, make):
        def body(d, _):
            make(d).start()
            return 0

        lax.fori_loop(1, count, body, 0)

    def wait_all(count, make):
        def body(d, _):
            make(d).wait()
            return 0

        lax.fori_loop(1, count, body, 0)

    load_b = pltpu.make_async_copy(
        b_hbm, bbuf.at[pl.ds(pl.multiple_of(h * brow, 8), brow)], lsem.at[hours]
    )
    load_c = pltpu.make_async_copy(c_hbm, cbuf, lsem.at[hours + 1])
    load_b.start()
    load_c.start()

    def load_t(i):
        return pltpu.make_async_copy(t_hbm.at[i], tbuf.at[i], lsem.at[i])

    def start_t(i, _):
        load_t(i).start()
        return 0

    lax.fori_loop(0, hours, start_t, 0)

    barrier = pltpu.get_barrier_semaphore()

    def greet(make):
        def body(d, _):
            pl.semaphore_signal(
                barrier, inc=1, device_id=make(d), device_id_type=MESH
            )
            return 0

        return body

    lax.fori_loop(1, Q, greet(plane), 0)
    lax.fori_loop(1, Z, greet(along_z), 0)
    pl.semaphore_signal(barrier, inc=1, device_id=other_core, device_id_type=MESH)
    pl.semaphore_wait(barrier, Q + Z - 1)

    base = 0

    my_b = pl.ds(pl.multiple_of(h * brow, 8), brow)
    send_b = lambda d: remote(bbuf.at[my_b], bbuf.at[my_b], d, along_hours(d))
    base += NH
    load_b.wait()
    start_all(NH, send_b)

    load_c.wait()
    c = cbuf[...]
    gc_part[...] = gram(c)
    hi = c.astype(bf16)
    chi[...] = hi
    clo[...] = (c - hi.astype(f32)).astype(bf16)
    my_rows = pl.ds(pl.multiple_of(half * core + prow * q, 8), prow)
    q_bins = h * NB + 1 - n
    bins_rows = pl.ds(pl.multiple_of(half * core + prow * q_bins, 8), prow)
    send_gc = remote(gc_part.at[bins_rows], gc_in, base, other_bins)
    base += 1
    send_gc.start()

    def contract(i, _):
        load_t(i).wait()
        x = tbuf[i]
        xh = x.astype(bf16)
        xl = (x - xh.astype(f32)).astype(bf16)
        dot = functools.partial(jnp.dot, preferred_element_type=f32)
        con[i] = dot(xh, chi[...]) + (dot(xh, clo[...]) + dot(xl, chi[...]))
        return 0

    wait_all(NH, send_b)
    gb_part[...] = gram(bbuf[...])
    core_rows = pl.ds(pl.multiple_of(half * (1 - core) + prow * q, 8), prow)
    send_gb = remote(gb_part.at[core_rows], gb_in, base, other_core)
    base += 1
    send_gb.start()

    send_gc.wait()
    gcm[my_rows, :] = gc_part[my_rows, :] + gc_in[...]
    gc_base = base
    send_gcm = lambda d: remote(gcm.at[my_rows], gcm.at[my_rows], gc_base + d, plane(d))
    base += Q
    start_all(Q, send_gcm)

    send_gb.wait()
    gb_z[z] = gb_part[my_rows, :] + gb_in[...]
    z_base = base
    send_gbz = lambda d: remote(gb_z.at[z], gb_z.at[z], z_base + d, along_z(d))
    base += Z
    start_all(Z, send_gbz)

    lax.fori_loop(0, hours // 2, contract, 0)

    wait_all(Z, send_gbz)
    total = gb_z[0]
    for s in range(1, Z):
        total = total + gb_z[s]
    hmat[my_rows, :] = total * gcm[my_rows, :]
    h_base = base
    send_h = lambda d: remote(hmat.at[my_rows], hmat.at[my_rows], h_base + d, plane(d))
    base += Q
    start_all(Q, send_h)

    lax.fori_loop(hours // 2, hours, contract, 0)

    wait_all(Q, send_h)
    my_half = pl.ds(pl.multiple_of(half * core, 8), half)
    swap_h = remote(hmat.at[my_half], hmat.at[my_half], base, other_core)
    base += 1
    swap_h.start()
    wait_all(Q, send_gcm)
    swap_gc = remote(gcm.at[my_half], gcm.at[my_half], base, other_core)
    base += 1
    swap_gc.start()

    def partial_hours(i, _):
        mh[pl.ds(i, 1), :] = jnp.sum(con[i] * bbuf[...], axis=0, keepdims=True)
        return 0

    lax.fori_loop(0, hours, partial_hours, 0)
    keep = pl.ds(pl.multiple_of(hh * core, 8), hh)
    give = pl.ds(pl.multiple_of(hh * (1 - core), 8), hh)
    send_mc = remote(mh.at[give], mh_core, base, other_core)
    base += 1
    send_mc.start()

    blocks = width // 8
    marks = [0, blocks // 8, blocks // 4, blocks * 5 // 8, blocks]

    def run(s):
        def body(k, _):
            eliminate(k, hmat)
            return 0

        lax.fori_loop(marks[s], marks[s + 1], body, 0)

    swap_h.wait()
    run(0)
    send_mc.wait()
    mh_mine[...] = mh[keep, :] + mh_core[...]
    send_mb = remote(mh_mine, mh_bins, base, other_bins)
    base += 1
    send_mb.start()
    run(1)
    send_mb.wait()
    mh_z[z] = mh_mine[...] + mh_bins[...]
    mz_base = base
    send_mz = lambda d: remote(mh_z.at[z], mh_z.at[z], mz_base + d, along_z(d))
    base += Z
    start_all(Z, send_mz)
    run(2)
    wait_all(Z, send_mz)
    total = mh_z[0]
    for s in range(1, Z):
        total = total + mh_z[s]
    mh_all[keep, :] = total
    swap_m = remote(mh_all.at[keep], mh_all.at[keep], base, other_core)
    base += 1
    swap_m.start()
    run(3)
    swap_m.wait()

    hf = jnp.dot(
        mh_all[...], hmat[...], precision=HIGHEST, preferred_element_type=f32
    )
    my_hours = pl.ds(pl.multiple_of(h * hours, 8), hours)
    hfall[my_hours, :] = hf
    hf_base = base
    send_hf = lambda d: remote(
        hfall.at[my_hours], hfall.at[my_hours], hf_base + d, along_hours(d)
    )
    base += NH
    start_all(NH, send_hf)
    hf_ref[...] = hf

    def piece(t):
        rows = pl.ds(pl.multiple_of(t * mrow, 8), mrow)
        acc = con[0, rows, :] * hf[0:1, :]
        for i in range(1, hours):
            acc = acc + con[i, rows, :] * hf[i : i + 1, :]
        return acc

    mp_base = base
    send_mp = lambda d: remote(mp.at[d], mp_in.at[d], mp_base + d, plane(d))
    base += Q

    def points_body(d, _):
        mp[d] = piece(lax.rem(q + d, Q))
        send_mp(d).start()
        return 0

    lax.fori_loop(1, Q, points_body, 0)
    mp_in[0] = piece(q)

    wait_all(NH, send_hf)
    swap_gc.wait()
    hmat[...] = gram(hfall[...]) * gcm[...]
    run(0)
    run(1)
    wait_all(Q, send_mp)
    total = mp_in[0]
    for s in range(1, Q):
        total = total + mp_in[s]
    mine = pl.ds(pl.multiple_of(n * mrow, 8), mrow)
    owned[mine, :] = total
    swap_o = remote(owned.at[mine], owned.at[mine], base, other_bins)
    base += 1
    swap_o.start()
    run(2)
    run(3)
    swap_o.wait()
    pf_ref[...] = jnp.dot(
        owned[...], hmat[...], precision=HIGHEST, preferred_element_type=f32
    )


def local(sizes, tensor, b_factor, c_factor):
    NP, NH, NB = sizes
    Z, Q = NP // 2, NH * NB
    hours, points, bins = tensor.shape
    width = c_factor.shape[1]
    brow = b_factor.shape[0]
    prow = width // (2 * Q)
    mrow = points // Q
    hh = hours // 2
    sems = NH + 1 + 1 + Q + Z + Q + 2 + 1 + 1 + Z + 1 + NH + Q + 1
    vm = lambda *shape: pltpu.VMEM(shape, f32)
    any_spec = pl.BlockSpec(memory_space=pl.ANY)
    vmem_spec = pl.BlockSpec(memory_space=pltpu.VMEM)
    return pl.pallas_call(
        functools.partial(kernel, sizes),
        out_shape=(
            jax.ShapeDtypeStruct((hours, width), f32),
            jax.ShapeDtypeStruct((brow, width), f32),
        ),
        in_specs=[any_spec] * 3,
        out_specs=(vmem_spec, vmem_spec),
        scratch_shapes=[
            vm(hours, points, bins),
            vm(hours, points, width),
            vm(bins, width),
            pltpu.VMEM((bins, width), bf16),
            pltpu.VMEM((bins, width), bf16),
            vm(points, width),
            vm(width, width),
            vm(width, width),
            vm(prow, width),
            vm(prow, width),
            vm(Z, prow, width),
            vm(width, width),
            vm(width, width),
            vm(hours, width),
            vm(hh, width),
            vm(hh, width),
            vm(hh, width),
            vm(Z, hh, width),
            vm(hours, width),
            vm(hours * NH, width),
            vm(Q, mrow, width),
            vm(Q, mrow, width),
            vm(brow, width),
            pltpu.SemaphoreType.DMA((hours + 2,)),
            pltpu.SemaphoreType.DMA((sems,)),
            pltpu.SemaphoreType.DMA((sems,)),
        ],
        compiler_params=pltpu.CompilerParams(
            collective_id=0,
            has_side_effects=True,
            vmem_limit_bytes=40 * 1024 * 1024,
        ),
    )(tensor, b_factor, c_factor)


def solution(mesh):
    sizes = (mesh.shape["pts"], mesh.shape["hrs"], mesh.shape["bins"])
    placed = (P("hrs", "pts", "bins"), P(("pts", "hrs"), None), P("bins", None))
    return jax.shard_map(
        functools.partial(local, sizes),
        mesh=mesh,
        in_specs=placed,
        out_specs=(P("hrs", None), P(("pts", "hrs"), None)),
        check_vma=False,
    )
```

time: 1450 us -> 87.1 us (0.06)
  waiting for transfers between devices: 1110 us -> 0 us
  blocking collectives: 153 us -> 0 us
  other arithmetic: 115 us -> 0 us
  Pallas kernels: 0 us -> 67.6 us
  matrix products: 32.9 us -> 0 us
  between operations: 16.8 us -> 0.66 us
    psum x3 -> x0, waiting for transfers between devices: 1090 us -> none  [the longest x1 1010 us: local(): lax.psum(jnp.dot(b_factor.T, b_factor, precision=highest), ('pts', 'hrs'))]
    psum x2 -> x0, blocking collectives: 118 us -> none  [the longest x1 109 us: local(): mttkrp_hours = lax.psum(mttkrp_hours, ('pts', 'bins'))]
    another operation x19 -> x0, other arithmetic: 109 us -> none  [the longest x13 68.7 us: normal_solve(): factor = jnp.linalg.cholesky(hadamard)]
    pallas_call x0 -> x1, Pallas kernels: none -> 67.6 us  [local(): pl.pallas_call(functools.partial(kernel, sizes), out_shape=(jax.ShapeDtyp...]
    all_gather x1 -> x0, blocking collectives: 34.8 us -> none  [local(): b_block = lax.all_gather(b_factor, 'hrs', axis=0, tiled=True)]
    dot_general x4 -> x0, matrix products: 29.3 us -> none  [the longest x1 24 us: local(): jnp.dot(tensor.reshape(hour_rows * point_rows, bin_rows), c_factor, preci...]
    unnamed x5 -> x0, waiting for transfers between devices: 16.5 us -> none
    unnamed x7 -> x9, local copies, waits for them, and re-layouts: 1.92 us -> 17.8 us
  transfers between devices with their start and end apart: 4 -> 0, of which waited for: 3 -> 0; matrix products, arithmetic and copies ran while one was open for 6% -> 0% of each run, Pallas kernels for 0% -> 0%
where the time goes in v1:
time: 87.1 us; the launch traced here: 86.1 us
  Pallas kernels  67.6 us (78%)
  local copies, waits for them, and re-layouts  17.8 us (20%)
    pallas_call x1, Pallas kernels, local(): pl.pallas_call(functools.partial(kernel, sizes), out_shape=(jax.ShapeDtyp...  67.6 us
    unnamed x9, local copies, waits for them, and re-layouts  17.8 us

profile of v1, /device:TPU:8, one launch (start us, length us, event | category | flops | bytes accessed | tf_op | source)
XLA Modules:
  0.0 86.1 jit_solution(8562366385959082890)
XLA Ops:
  0.6 0.0 copy-start.1
  0.6 0.0 copy-start.2
  0.6 11.9 %copy.5.t_hbm = f32[16,256,648]{2,1,0:T(8,128)} copy(f32[16,256,648]{1,2,0:T(8,128)} %param.3) | data formatting | bytes 21233664 | tf_op args[0]
  12.6 0.0 copy-done.1
  12.6 0.0 copy-done.2
  12.6 0.0 copy-start
  12.6 4.6 %copy-done = f32[16,256,648]{2,1,0:T(8,128)S(1)} copy-done((f32[16,256,648]{2,1,0:T(8,128)S(1)}, f32[16,256,648]{2,1,0:T(8,128)}, u32[]{:S(2)}) %copy-start) | copy-done | bytes 10616856
  17.2 67.6 %shard_map.50 = (f32[16,256]{1,0:T(8,128)S(1)}, f32[32,256]{1,0:T(8,128)S(1)}) custom-call(f32[16,256,648]{2,1,0:T(8,128)S(1)} %copy-done, f32[32,256]{1,0:T(8,128)S(1)} %copy-done.2, f32[648,256]{1,0:T(8,128)S(1)} %copy-done.1), custom_call_target="tpu_custom_call" | custom-call | tf_op jit(solution)/shard_map/pallas_call | solution.py:379
  84.8 0.6 copy.8
  85.4 0.6 copy.9
Async XLA Ops:
  0.6 12.0 %copy-start.1 = (f32[648,256]{1,0:T(8,128)S(1)}, f32[648,256]{1,0:T(8,128)}, u32[]{:S(2)}) copy-start(f32[648,256]{1,0:T(8,128)} %c_hbm.1) | copy-start | bytes 1990660
  0.6 12.0 %copy-start.2 = (f32[32,256]{1,0:T(8,128)S(1)}, f32[32,256]{1,0:T(8,128)}, u32[]{:S(2)}) copy-start(f32[32,256]{1,0:T(8,128)} %b_hbm.1) | copy-start | bytes 98308
  12.6 4.6 %copy-start = (f32[16,256,648]{2,1,0:T(8,128)S(1)}, f32[16,256,648]{2,1,0:T(8,128)}, u32[]{:S(2)}) copy-start(f32[16,256,648]{2,1,0:T(8,128)} %copy.5.t_hbm) | copy-start | bytes 31850500

commit v2 on v1

--- a/solution.py
+++ b/solution.py
@@ -27,48 +27,110 @@
     return first, second, rest - second
 
 
-def reciprocal(x):
-    y = pltpu.reciprocal(x, approx=True)
-    y = y * (2.0 - x * y)
-    return y * (2.0 - x * y)
-
-
-def eliminate(k, a):
-    width = a.shape[1]
-    row = pl.multiple_of(k * 8, 8)
-    panel = a[pl.ds(row, 8), :]
-    tile = pl.multiple_of((k // 16) * 128, 128)
-    pivots = pltpu.roll(
-        a[pl.ds(row, 8), pl.ds(tile, 128)], lax.rem(128 - lax.rem(k, 16) * 8, 128), 1
-    )
-    lane = lax.broadcasted_iota(jnp.int32, (8, width), 1)
-    sub = lax.broadcasted_iota(jnp.int32, (8, width), 0)
-    sub1 = lax.broadcasted_iota(jnp.int32, (8, 128), 0)
+STEP = 16
+
+
+def spread_lanes(x, first):
+    return [
+        jnp.take_along_axis(
+            x,
+            jnp.full(x.shape, first + j, jnp.int32),
+            axis=1,
+            mode="promise_in_bounds",
+        )
+        for j in range(STEP)
+    ]
+
+
+def spread_row(x, j):
+    return jnp.broadcast_to(x[j : j + 1, :], x.shape)
+
+
+def lane_tile(x, t):
+    return jnp.where(t == 0, x[:, :128], x[:, 128:])
+
+
+def pivot(panel, row):
+    lane = lax.broadcasted_iota(jnp.int32, panel.shape, 1)
+    sub = lax.broadcasted_iota(jnp.int32, panel.shape, 0)
     rel = lane - row
-    inside = (rel >= 0) & (rel < 8)
+    t = row // 128
+    cols = spread_lanes(lane_tile(panel, t), row - t * 128)
+    work = jnp.where((rel >= 0) & (rel < STEP), jnp.where(rel == sub, 1.0, 0.0), panel)
+    data = [work[:, :128], work[:, 128:]]
+    sub = lax.broadcasted_iota(jnp.int32, (STEP, 128), 0)
+    for j in range(STEP):
+        state = cols[j:] + data
+        rows = [spread_row(x, j) for x in state]
+        inverse = pltpu.reciprocal(rows[0], approx=False)
+        factor = jnp.where(sub == j, 1.0 - inverse, cols[j] * inverse)
+        state = [x - factor * r for x, r in zip(state, rows)]
+        cols = cols[:j] + state[: STEP - j]
+        data = state[STEP - j :]
     column = jnp.where(lane < row, -panel, panel)
-    work = jnp.where(inside, jnp.where(rel == sub, 1.0, 0.0), panel)
-    cols = [jnp.broadcast_to(pivots[:, j : j + 1], (8, 128)) for j in range(8)]
-    data = [work[:, s : s + 128] for s in range(0, width, 128)]
-    for j in range(8):
-        state = cols[j:] + data
-        rows = [jnp.broadcast_to(x[j : j + 1, :], (8, 128)) for x in state]
-        inverse = reciprocal(rows[0])
-        factor = jnp.where(sub1 == j, 1.0 - inverse, cols[j] * inverse)
-        state = [x - factor * r for x, r in zip(state, rows)]
-        cols = cols[:j] + state[: 8 - j]
-        data = state[8 - j :]
-    panel = jnp.concatenate(data, axis=1)
+    return jnp.concatenate(data, axis=1), column
+
+
+def follow(rows, done, row):
+    rel = lax.broadcasted_iota(jnp.int32, rows.shape, 1) - row
+    t = row // 128
+    cols = spread_lanes(lane_tile(rows, t), row - t * 128)
+    rows = jnp.where((rel >= 0) & (rel < STEP), 0.0, rows)
+    out = []
+    for s in (0, 128):
+        part = done[:, s : s + 128]
+        terms = [cols[j] * spread_row(part, j) for j in range(STEP)]
+        while len(terms) > 1:
+            terms = [x + y for x, y in zip(terms[::2], terms[1::2])]
+        out.append(rows[:, s : s + 128] - terms[0])
+    return jnp.concatenate(out, axis=1)
+
+
+def factors(left, right, column, done):
     c1, c2, c3 = split(column)
-    r1, r2, r3 = split(panel)
-    left = jnp.concatenate([c1, c1, c2, c2, c1, c3], axis=0).astype(bf16)
-    right = jnp.concatenate([r1, r2, r1, r2, r3, r1], axis=0).astype(bf16)
+    r1, r2, r3 = split(done)
+    left[...] = jnp.concatenate([c1, c1, c2, c2, c1, c3], axis=0).astype(bf16)
+    right[...] = jnp.concatenate([r1, r2, r1, r2, r3, r1], axis=0).astype(bf16)
+
+
+def late_update(a, left, right, row, done):
     update = lax.dot_general(
-        left, right, CONTRACT_ROWS, preferred_element_type=f32
+        left[...], right[...], CONTRACT_ROWS, preferred_element_type=f32
     )
     rel = lax.broadcasted_iota(jnp.int32, a.shape, 1) - row
-    a[...] = jnp.where((rel >= 0) & (rel < 8), 0.0, a[...]) - update
-    a[pl.ds(row, 8), :] = panel
+    a[...] = jnp.where((rel >= 0) & (rel < STEP), 0.0, a[...]) - update
+    a[pl.ds(row, STEP), :] = done
+
+
+def invert(a, left, right, pauses):
+    steps = a.shape[0] // STEP
+
+    def at(k):
+        return pl.multiple_of(k * STEP, STEP)
+
+    done, column = pivot(a[0:STEP, :], 0)
+    factors(left, right, column, done)
+    panel = follow(a[STEP : 2 * STEP, :], done, 0)
+
+    def body(k, carry):
+        panel, before = carry
+        late_update(a, left, right, at(k - 1), before)
+        done, column = pivot(panel, at(k))
+        panel = follow(a[pl.ds(at(k + 1), STEP), :], done, at(k))
+        factors(left, right, column, done)
+        return panel, done
+
+    carry = (panel, done)
+    first = 1
+    for stop in sorted(pauses):
+        carry = lax.fori_loop(first, stop, body, carry)
+        pauses[stop]()
+        first = stop
+    panel, before = lax.fori_loop(first, steps - 1, body, carry)
+    late_update(a, left, right, at(steps - 2), before)
+    done, column = pivot(panel, at(steps - 1))
+    factors(left, right, column, done)
+    late_update(a, left, right, at(steps - 1), done)
 
 
 def kernel(
@@ -81,9 +143,9 @@
     tbuf,
     con,
     cbuf,
-    chi,
-    clo,
+    ct,
     bbuf,
+    bt,
     gb_part,
     gc_part,
     gb_in,
@@ -91,23 +153,28 @@
     gb_z,
     hmat,
     gcm,
+    mht,
     mh,
     mh_core,
     mh_mine,
     mh_bins,
     mh_z,
     mh_all,
+    hft,
     hfall,
+    mpt,
     mp,
     mp_in,
     owned,
+    left,
+    right,
     lsem,
     ssem,
     rsem,
 ):
     NP, NH, NB = sizes
     Z, Q = NP // 2, NH * NB
-    hours, points, _ = t_hbm.shape
+    hours, _, points = t_hbm.shape
     width = c_hbm.shape[1]
     half = width // 2
     prow = half // Q
@@ -196,17 +263,17 @@
     start_all(NH, send_b)
 
     load_c.wait()
-    c = cbuf[...]
-    gc_part[...] = gram(c)
-    hi = c.astype(bf16)
-    chi[...] = hi
-    clo[...] = (c - hi.astype(f32)).astype(bf16)
+    gc_part[...] = gram(cbuf[...])
     my_rows = pl.ds(pl.multiple_of(half * core + prow * q, 8), prow)
     q_bins = h * NB + 1 - n
     bins_rows = pl.ds(pl.multiple_of(half * core + prow * q_bins, 8), prow)
     send_gc = remote(gc_part.at[bins_rows], gc_in, base, other_bins)
     base += 1
     send_gc.start()
+    c = cbuf[...].T
+    hi = c.astype(bf16)
+    ct[:width, :] = hi
+    ct[width:, :] = (c - hi.astype(f32)).astype(bf16)
 
     def contract(i, _):
         load_t(i).wait()
@@ -214,11 +281,13 @@
         xh = x.astype(bf16)
         xl = (x - xh.astype(f32)).astype(bf16)
         dot = functools.partial(jnp.dot, preferred_element_type=f32)
-        con[i] = dot(xh, chi[...]) + (dot(xh, clo[...]) + dot(xl, chi[...]))
+        chi, clo = ct[:width, :], ct[width:, :]
+        con[i] = dot(chi, xh) + (dot(clo, xh) + dot(chi, xl))
         return 0
 
     wait_all(NH, send_b)
     gb_part[...] = gram(bbuf[...])
+    bt[...] = bbuf[...].T
     core_rows = pl.ds(pl.multiple_of(half * (1 - core) + prow * q, 8), prow)
     send_gb = remote(gb_part.at[core_rows], gb_in, base, other_core)
     base += 1
@@ -262,51 +331,50 @@
     base += 1
     swap_gc.start()
 
+    lane = lax.broadcasted_iota(jnp.int32, mht.shape, 1)
+
     def partial_hours(i, _):
-        mh[pl.ds(i, 1), :] = jnp.sum(con[i] * bbuf[...], axis=0, keepdims=True)
+        prod = con[i] * bt[...]
+        total = jnp.sum(prod, axis=1, keepdims=True)
+        mht[...] = jnp.where(lane == i, total, mht[...])
         return 0
 
     lax.fori_loop(0, hours, partial_hours, 0)
+    mh[...] = mht[...].T[:hours, :]
     keep = pl.ds(pl.multiple_of(hh * core, 8), hh)
     give = pl.ds(pl.multiple_of(hh * (1 - core), 8), hh)
     send_mc = remote(mh.at[give], mh_core, base, other_core)
     base += 1
     send_mc.start()
 
-    blocks = width // 8
-    marks = [0, blocks // 8, blocks // 4, blocks * 5 // 8, blocks]
-
-    def run(s):
-        def body(k, _):
-            eliminate(k, hmat)
-            return 0
-
-        lax.fori_loop(marks[s], marks[s + 1], body, 0)
-
-    swap_h.wait()
-    run(0)
-    send_mc.wait()
-    mh_mine[...] = mh[keep, :] + mh_core[...]
     send_mb = remote(mh_mine, mh_bins, base, other_bins)
     base += 1
-    send_mb.start()
-    run(1)
-    send_mb.wait()
-    mh_z[z] = mh_mine[...] + mh_bins[...]
     mz_base = base
     send_mz = lambda d: remote(mh_z.at[z], mh_z.at[z], mz_base + d, along_z(d))
     base += Z
-    start_all(Z, send_mz)
-    run(2)
-    wait_all(Z, send_mz)
-    total = mh_z[0]
-    for s in range(1, Z):
-        total = total + mh_z[s]
-    mh_all[keep, :] = total
     swap_m = remote(mh_all.at[keep], mh_all.at[keep], base, other_core)
     base += 1
-    swap_m.start()
-    run(3)
+
+    def pause_core():
+        send_mc.wait()
+        mh_mine[...] = mh[keep, :] + mh_core[...]
+        send_mb.start()
+
+    def pause_bins():
+        send_mb.wait()
+        mh_z[z] = mh_mine[...] + mh_bins[...]
+        start_all(Z, send_mz)
+
+    def pause_z():
+        wait_all(Z, send_mz)
+        total = mh_z[0]
+        for s in range(1, Z):
+            total = total + mh_z[s]
+        mh_all[keep, :] = total
+        swap_m.start()
+
+    swap_h.wait()
+    invert(hmat, left, right, {3: pause_core, 6: pause_bins, 11: pause_z})
     swap_m.wait()
 
     hf = jnp.dot(
@@ -314,6 +382,7 @@
     )
     my_hours = pl.ds(pl.multiple_of(h * hours, 8), hours)
     hfall[my_hours, :] = hf
+    hft[...] = hf.T
     hf_base = base
     send_hf = lambda d: remote(
         hfall.at[my_hours], hfall.at[my_hours], hf_base + d, along_hours(d)
@@ -322,41 +391,40 @@
     start_all(NH, send_hf)
     hf_ref[...] = hf
 
-    def piece(t):
+    chunk = 32
+    for rows in range(0, width, chunk):
+        weights = hft[rows : rows + chunk, :]
+        acc = con[0, rows : rows + chunk, :] * weights[:, 0:1]
+        for i in range(1, hours):
+            acc = acc + con[i, rows : rows + chunk, :] * weights[:, i : i + 1]
+        mpt[rows : rows + chunk, :] = acc
+    mp[...] = mpt[...].T
+    mp_base = base
+
+    def send_mp(d):
+        t = lax.rem(q + d, Q)
         rows = pl.ds(pl.multiple_of(t * mrow, 8), mrow)
-        acc = con[0, rows, :] * hf[0:1, :]
-        for i in range(1, hours):
-            acc = acc + con[i, rows, :] * hf[i : i + 1, :]
-        return acc
-
-    mp_base = base
-    send_mp = lambda d: remote(mp.at[d], mp_in.at[d], mp_base + d, plane(d))
+        return remote(mp.at[rows], mp_in.at[d], mp_base + d, plane(d))
+
     base += Q
-
-    def points_body(d, _):
-        mp[d] = piece(lax.rem(q + d, Q))
-        send_mp(d).start()
-        return 0
-
-    lax.fori_loop(1, Q, points_body, 0)
-    mp_in[0] = piece(q)
+    start_all(Q, send_mp)
 
     wait_all(NH, send_hf)
     swap_gc.wait()
     hmat[...] = gram(hfall[...]) * gcm[...]
-    run(0)
-    run(1)
-    wait_all(Q, send_mp)
-    total = mp_in[0]
-    for s in range(1, Q):
-        total = total + mp_in[s]
     mine = pl.ds(pl.multiple_of(n * mrow, 8), mrow)
-    owned[mine, :] = total
     swap_o = remote(owned.at[mine], owned.at[mine], base, other_bins)
     base += 1
-    swap_o.start()
-    run(2)
-    run(3)
+
+    def pause_points():
+        wait_all(Q, send_mp)
+        total = mp[pl.ds(pl.multiple_of(q * mrow, 8), mrow), :]
+        for s in range(1, Q):
+            total = total + mp_in[s]
+        owned[mine, :] = total
+        swap_o.start()
+
+    invert(hmat, left, right, {8: pause_points})
     swap_o.wait()
     pf_ref[...] = jnp.dot(
         owned[...], hmat[...], precision=HIGHEST, preferred_element_type=f32
@@ -366,7 +434,8 @@
 def local(sizes, tensor, b_factor, c_factor):
     NP, NH, NB = sizes
     Z, Q = NP // 2, NH * NB
-    hours, points, bins = tensor.shape
+    tensor = jnp.swapaxes(tensor, 1, 2)
+    hours, bins, points = tensor.shape
     width = c_factor.shape[1]
     brow = b_factor.shape[0]
     prow = width // (2 * Q)
@@ -374,7 +443,7 @@
     hh = hours // 2
     sems = NH + 1 + 1 + Q + Z + Q + 2 + 1 + 1 + Z + 1 + NH + Q + 1
     vm = lambda *shape: pltpu.VMEM(shape, f32)
-    any_spec = pl.BlockSpec(memory_space=pl.ANY)
+    any_spec = pl.BlockSpec(memory_space=pltpu.HBM)
     vmem_spec = pl.BlockSpec(memory_space=pltpu.VMEM)
     return pl.pallas_call(
         functools.partial(kernel, sizes),
@@ -385,12 +454,12 @@
         in_specs=[any_spec] * 3,
         out_specs=(vmem_spec, vmem_spec),
         scratch_shapes=[
-            vm(hours, points, bins),
-            vm(hours, points, width),
+            vm(hours, bins, points),
+            vm(hours, width, points),
             vm(bins, width),
-            pltpu.VMEM((bins, width), bf16),
-            pltpu.VMEM((bins, width), bf16),
+            pltpu.VMEM((2 * width, bins), bf16),
             vm(points, width),
+            vm(width, points),
             vm(width, width),
             vm(width, width),
             vm(prow, width),
@@ -398,16 +467,21 @@
             vm(Z, prow, width),
             vm(width, width),
             vm(width, width),
+            vm(width, 128),
             vm(hours, width),
             vm(hh, width),
             vm(hh, width),
             vm(hh, width),
             vm(Z, hh, width),
             vm(hours, width),
+            vm(width, hours),
             vm(hours * NH, width),
-            vm(Q, mrow, width),
+            vm(width, points),
+            vm(points, width),
             vm(Q, mrow, width),
             vm(brow, width),
+            pltpu.VMEM((6 * STEP, width), bf16),
+            pltpu.VMEM((6 * STEP, width), bf16),
             pltpu.SemaphoreType.DMA((hours + 2,)),
             pltpu.SemaphoreType.DMA((sems,)),
             pltpu.SemaphoreType.DMA((sems,)),
@@ -415,7 +489,7 @@
         compiler_params=pltpu.CompilerParams(
             collective_id=0,
             has_side_effects=True,
-            vmem_limit_bytes=40 * 1024 * 1024,
+            vmem_limit_bytes=56 * 1024 * 1024,
         ),
     )(tensor, b_factor, c_factor)
 

time: 87.1 us -> 59.3 us (0.68)
  local copies, waits for them, and re-layouts: 17.8 us -> 2.7 us
  Pallas kernels: 67.6 us -> 55.7 us
    unnamed x9 -> x2, local copies, waits for them, and re-layouts: 17.8 us -> 2.7 us
    pallas_call x1, Pallas kernels: 67.6 us -> 55.7 us  [local(): pl.pallas_call(functools.partial(kernel, sizes), out_shape=(jax.ShapeDtyp...]
where the time goes in v2:
time: 59.3 us; the launch traced here: 59 us
  Pallas kernels  55.7 us (94%)
  local copies, waits for them, and re-layouts  2.7 us (5%)
  between operations  0.64 us (1%)
    pallas_call x1, Pallas kernels, local(): pl.pallas_call(functools.partial(kernel, sizes), out_shape=(jax.ShapeDtyp...  55.7 us
    unnamed x2, local copies, waits for them, and re-layouts  2.7 us

profile of v2, /device:TPU:8, one launch (start us, length us, event | category | flops | bytes accessed | tf_op | source)
XLA Modules:
  0.0 59.0 jit_solution(14459303871194497846)
XLA Ops:
  0.6 55.7 %shard_map.50 = (f32[16,256]{1,0:T(8,128)}, f32[32,256]{1,0:T(8,128)}) custom-call(f32[16,648,256]{2,1,0:T(8,128)} %bitcast.1, f32[32,256]{1,0:T(8,128)} %b_hbm.1, f32[648,256]{1,0:T(8,128)} %c_hbm.1), custom_call_target="tpu_custom_call" | custom-call | tf_op jit(solution)/shard_map/pallas_call | solution.py:448
  56.3 1.3 %copy.7 = f32[16,256]{1,0:T(8,128)} copy(f32[16,256]{1,0:T(8,128)} %get-tuple-element.4) | data formatting | bytes 32768
  57.7 1.4 %copy.8 = f32[32,256]{1,0:T(8,128)} copy(f32[32,256]{1,0:T(8,128)} %get-tuple-element.5) | data formatting | bytes 65536

commit v3 on v2

--- a/solution.py
+++ b/solution.py
@@ -14,10 +14,21 @@
 CONTRACT_ROWS = (((0,), (0,)), ((), ()))
 
 
+def dot(a, b, dims):
+    return lax.dot_general(a, b, (dims, ((), ())), preferred_element_type=f32)
+
+
+def halves(x):
+    hi = x.astype(bf16)
+    return hi, (x - hi.astype(f32)).astype(bf16)
+
+
 def gram(x):
-    return lax.dot_general(
-        x, x, CONTRACT_ROWS, precision=HIGHEST, preferred_element_type=f32
-    )
+    hi = x.astype(bf16).astype(f32)
+    lo = x - hi
+    left = jnp.concatenate([hi, hi, lo, lo], axis=0).astype(bf16)
+    right = jnp.concatenate([hi, lo, hi, lo], axis=0).astype(bf16)
+    return dot(left, right, ((0,), (0,)))
 
 
 def split(x):
@@ -145,19 +156,18 @@
     cbuf,
     ct,
     bbuf,
+    bx,
     bt,
     gb_part,
+    gb_in,
+    gb_z,
     gc_part,
-    gb_in,
     gc_in,
-    gb_z,
     hmat,
     gcm,
     mht,
     mh,
-    mh_core,
-    mh_mine,
-    mh_bins,
+    mh_in,
     mh_z,
     mh_all,
     hft,
@@ -173,27 +183,52 @@
     rsem,
 ):
     NP, NH, NB = sizes
-    Z, Q = NP // 2, NH * NB
+    Z, Q, NX = NP // 2, NH * NB, NH // 2
+    YC = 8
     hours, _, points = t_hbm.shape
     width = c_hbm.shape[1]
     half = width // 2
     prow = half // Q
     brow = b_hbm.shape[0]
+    bhalf = brow // 2
     mrow = points // Q
     hh = hours // 2
     p, h, n = lax.axis_index("pts"), lax.axis_index("hrs"), lax.axis_index("bins")
     z, core = p // 2, lax.rem(p, 2)
+    y_hi, x = h // NX, lax.rem(h, NX)
     q = h * NB + n
+    w = (2 * y_hi + n) * 2 + core
+    g = 2 * core + n
 
     def plane(d):
         t = lax.rem(q + d, Q)
         return (p, t // NB, lax.rem(t, NB))
 
-    def along_hours(d):
-        return (p, lax.rem(h + d, NH), n)
+    def along_x(d):
+        return (p, y_hi * NX + lax.rem(x + d, NX), n)
+
+    def hour_block(d):
+        flip = d // NX
+        return (
+            p,
+            lax.rem(y_hi + flip, 2) * NX + lax.rem(x + d, NX),
+            lax.rem(n + flip, 2),
+        )
 
     def along_z(d):
         return (lax.rem(z + d, Z) * 2 + core, h, n)
+
+    def split_w(d):
+        t = lax.rem(w + d, YC)
+        return t // 4, lax.rem(t // 2, 2), lax.rem(t, 2)
+
+    def column(d):
+        y2, n2, core2 = split_w(d)
+        return (z * 2 + core2, y2 * NX + x, n2)
+
+    def quad(d):
+        t = lax.rem(g + d, 4)
+        return (z * 2 + t // 2, h, lax.rem(t, 2))
 
     other_core = (p + 1 - 2 * core, h, n)
     other_bins = (p, h, 1 - n)
@@ -208,23 +243,32 @@
             device_id_type=MESH,
         )
 
-    def start_all(count, make):
+    def start_all(count, make, first=1):
         def body(d, _):
             make(d).start()
             return 0
 
-        lax.fori_loop(1, count, body, 0)
-
-    def wait_all(count, make):
+        lax.fori_loop(first, count, body, 0)
+
+    def wait_all(count, make, first=1):
         def body(d, _):
             make(d).wait()
             return 0
 
-        lax.fori_loop(1, count, body, 0)
-
-    load_b = pltpu.make_async_copy(
-        b_hbm, bbuf.at[pl.ds(pl.multiple_of(h * brow, 8), brow)], lsem.at[hours]
-    )
+        lax.fori_loop(first, count, body, 0)
+
+    def at(i, size):
+        return pl.ds(pl.multiple_of(i * size, 8), size)
+
+    base = 0
+
+    def take(count):
+        nonlocal base
+        base += count
+        return base - count
+
+    my_b = at(h, brow)
+    load_b = pltpu.make_async_copy(b_hbm, bbuf.at[my_b], lsem.at[hours])
     load_c = pltpu.make_async_copy(c_hbm, cbuf, lsem.at[hours + 1])
     load_b.start()
     load_c.start()
@@ -251,144 +295,183 @@
 
     lax.fori_loop(1, Q, greet(plane), 0)
     lax.fori_loop(1, Z, greet(along_z), 0)
-    pl.semaphore_signal(barrier, inc=1, device_id=other_core, device_id_type=MESH)
-    pl.semaphore_wait(barrier, Q + Z - 1)
-
-    base = 0
-
-    my_b = pl.ds(pl.multiple_of(h * brow, 8), brow)
-    send_b = lambda d: remote(bbuf.at[my_b], bbuf.at[my_b], d, along_hours(d))
-    base += NH
+
+    def greet_column(i, _):
+        pl.semaphore_signal(
+            barrier,
+            inc=1,
+            device_id=(z * 2 + 1 - core, (i // 2) * NX + x, lax.rem(i, 2)),
+            device_id_type=MESH,
+        )
+        return 0
+
+    lax.fori_loop(0, YC // 2, greet_column, 0)
+    pl.semaphore_wait(barrier, Q - 1 + Z - 1 + YC // 2)
+
     load_b.wait()
-    start_all(NH, send_b)
+    bx[at(x, bhalf), :] = bbuf[pl.ds(pl.multiple_of(h * brow + n * bhalf, 8), bhalf), :]
+    x_base = take(NX)
+    send_x = lambda d: remote(
+        bx.at[at(x, bhalf)], bx.at[at(x, bhalf)], x_base + d, along_x(d)
+    )
+    start_all(NX, send_x)
 
     load_c.wait()
-    gc_part[...] = gram(cbuf[...])
-    my_rows = pl.ds(pl.multiple_of(half * core + prow * q, 8), prow)
-    q_bins = h * NB + 1 - n
-    bins_rows = pl.ds(pl.multiple_of(half * core + prow * q_bins, 8), prow)
-    send_gc = remote(gc_part.at[bins_rows], gc_in, base, other_bins)
-    base += 1
-    send_gc.start()
-    c = cbuf[...].T
-    hi = c.astype(bf16)
-    ct[:width, :] = hi
-    ct[width:, :] = (c - hi.astype(f32)).astype(bf16)
+    chi, clo = halves(cbuf[...].T)
+    ct[:width, :] = chi
+    ct[width:, :] = clo
 
     def contract(i, _):
         load_t(i).wait()
-        x = tbuf[i]
-        xh = x.astype(bf16)
-        xl = (x - xh.astype(f32)).astype(bf16)
-        dot = functools.partial(jnp.dot, preferred_element_type=f32)
+        thi, tlo = halves(tbuf[i])
         chi, clo = ct[:width, :], ct[width:, :]
-        con[i] = dot(chi, xh) + (dot(clo, xh) + dot(chi, xl))
+        mul = functools.partial(dot, dims=((1,), (0,)))
+        con[i] = mul(chi, thi) + (mul(clo, thi) + mul(chi, tlo))
         return 0
 
-    wait_all(NH, send_b)
-    gb_part[...] = gram(bbuf[...])
-    bt[...] = bbuf[...].T
-    core_rows = pl.ds(pl.multiple_of(half * (1 - core) + prow * q, 8), prow)
-    send_gb = remote(gb_part.at[core_rows], gb_in, base, other_core)
-    base += 1
-    send_gb.start()
-
+    def contract_hours(first, last):
+        lax.fori_loop(first * hours // 16, last * hours // 16, contract, 0)
+
+    contract_hours(0, 1)
+
+    wait_all(NX, send_x)
+    gb_part[...] = gram(bx[...])
+    my_rows = pl.ds(pl.multiple_of(half * core + prow * q, 8), prow)
+    col_base = take(YC)
+
+    def send_col(d):
+        y2, n2, core2 = split_w(d)
+        q2 = (y2 * NX + x) * NB + n2
+        rows = pl.ds(pl.multiple_of(half * core2 + prow * q2, 8), prow)
+        return remote(gb_part.at[rows], gb_in.at[w], col_base + d, column(d))
+
+    start_all(YC, send_col)
+    gb_in[w] = gb_part[my_rows, :]
+
+    chi, clo = ct[:width, :], ct[width:, :]
+    mul = functools.partial(dot, dims=((1,), (1,)))
+    gc_part[...] = mul(chi, chi) + (mul(chi, clo) + mul(clo, chi))
+    bins_rows = pl.ds(
+        pl.multiple_of(half * core + prow * (h * NB + 1 - n), 8), prow
+    )
+    send_gc = remote(gc_part.at[bins_rows], gc_in, take(1), other_bins)
+    send_gc.start()
+    contract_hours(1, 3)
+
+    def add_up(ref, count):
+        total = ref[0]
+        for s in range(1, count):
+            total = total + ref[s]
+        return total
+
+    wait_all(YC, send_col)
+    gb_z[z] = add_up(gb_in, YC)
+    z_base = take(Z)
+    send_gbz = lambda d: remote(gb_z.at[z], gb_z.at[z], z_base + d, along_z(d))
+    start_all(Z, send_gbz)
+    contract_hours(3, 7)
+
+    wait_all(Z, send_gbz)
     send_gc.wait()
     gcm[my_rows, :] = gc_part[my_rows, :] + gc_in[...]
-    gc_base = base
-    send_gcm = lambda d: remote(gcm.at[my_rows], gcm.at[my_rows], gc_base + d, plane(d))
-    base += Q
+    hmat[my_rows, :] = add_up(gb_z, Z) * gcm[my_rows, :]
+    h_base = take(Q)
+    send_h = lambda d: remote(hmat.at[my_rows], hmat.at[my_rows], h_base + d, plane(d))
+    start_all(Q, send_h)
+
+    bx_base = take(NX)
+    b_other = pl.ds(pl.multiple_of(h * brow + (1 - n) * bhalf, 8), bhalf)
+    send_b2 = lambda d: remote(
+        bbuf.at[b_other], bbuf.at[b_other], bx_base + d, along_x(d)
+    )
+    b_base = take(NH)
+    send_b = lambda d: remote(bbuf.at[my_b], bbuf.at[my_b], b_base + d, hour_block(d))
+    start_all(NX, send_b2)
+    start_all(NH, send_b, NX)
+    contract_hours(7, 13)
+
+    wait_all(Q, send_h)
+    my_half = at(core, half)
+    swap_h = remote(hmat.at[my_half], hmat.at[my_half], take(1), other_core)
+    swap_h.start()
+    gc_base = take(Q)
+    send_gcm = lambda d: remote(
+        gcm.at[my_rows], gcm.at[my_rows], gc_base + d, plane(d)
+    )
     start_all(Q, send_gcm)
-
-    send_gb.wait()
-    gb_z[z] = gb_part[my_rows, :] + gb_in[...]
-    z_base = base
-    send_gbz = lambda d: remote(gb_z.at[z], gb_z.at[z], z_base + d, along_z(d))
-    base += Z
-    start_all(Z, send_gbz)
-
-    lax.fori_loop(0, hours // 2, contract, 0)
-
-    wait_all(Z, send_gbz)
-    total = gb_z[0]
-    for s in range(1, Z):
-        total = total + gb_z[s]
-    hmat[my_rows, :] = total * gcm[my_rows, :]
-    h_base = base
-    send_h = lambda d: remote(hmat.at[my_rows], hmat.at[my_rows], h_base + d, plane(d))
-    base += Q
-    start_all(Q, send_h)
-
-    lax.fori_loop(hours // 2, hours, contract, 0)
-
-    wait_all(Q, send_h)
-    my_half = pl.ds(pl.multiple_of(half * core, 8), half)
-    swap_h = remote(hmat.at[my_half], hmat.at[my_half], base, other_core)
-    base += 1
-    swap_h.start()
-    wait_all(Q, send_gcm)
-    swap_gc = remote(gcm.at[my_half], gcm.at[my_half], base, other_core)
-    base += 1
-    swap_gc.start()
-
+    contract_hours(13, 16)
+
+    wait_all(NX, send_b2)
+    wait_all(NH, send_b, NX)
+
+    def own_rows(d, _):
+        rows = pl.ds(
+            pl.multiple_of((y_hi * NX + d) * brow + n * bhalf, 8), bhalf
+        )
+        bbuf[rows, :] = bx[at(d, bhalf), :]
+        return 0
+
+    lax.fori_loop(0, NX, own_rows, 0)
+    bt[...] = bbuf[...].T
     lane = lax.broadcasted_iota(jnp.int32, mht.shape, 1)
 
     def partial_hours(i, _):
-        prod = con[i] * bt[...]
-        total = jnp.sum(prod, axis=1, keepdims=True)
+        total = jnp.sum(con[i] * bt[...], axis=1, keepdims=True)
         mht[...] = jnp.where(lane == i, total, mht[...])
         return 0
 
     lax.fori_loop(0, hours, partial_hours, 0)
     mh[...] = mht[...].T[:hours, :]
-    keep = pl.ds(pl.multiple_of(hh * core, 8), hh)
-    give = pl.ds(pl.multiple_of(hh * (1 - core), 8), hh)
-    send_mc = remote(mh.at[give], mh_core, base, other_core)
-    base += 1
-    send_mc.start()
-
-    send_mb = remote(mh_mine, mh_bins, base, other_bins)
-    base += 1
-    mz_base = base
+
+    def tile(c2, n2):
+        return at(c2, hh), pl.ds(pl.multiple_of(n2 * half, 128), half)
+
+    my_tile = tile(core, n)
+    mq_base = take(4)
+
+    def send_mq(d):
+        t = lax.rem(g + d, 4)
+        return remote(
+            mh.at[tile(t // 2, lax.rem(t, 2))], mh_in.at[g], mq_base + d, quad(d)
+        )
+
+    start_all(4, send_mq)
+    mh_in[g] = mh[my_tile]
+    mz_base = take(Z)
     send_mz = lambda d: remote(mh_z.at[z], mh_z.at[z], mz_base + d, along_z(d))
-    base += Z
-    swap_m = remote(mh_all.at[keep], mh_all.at[keep], base, other_core)
-    base += 1
-
-    def pause_core():
-        send_mc.wait()
-        mh_mine[...] = mh[keep, :] + mh_core[...]
-        send_mb.start()
-
-    def pause_bins():
-        send_mb.wait()
-        mh_z[z] = mh_mine[...] + mh_bins[...]
+    ma_base = take(4)
+    send_ma = lambda d: remote(
+        mh_all.at[my_tile], mh_all.at[my_tile], ma_base + d, quad(d)
+    )
+
+    def pause_quad():
+        wait_all(4, send_mq)
+        mh_z[z] = add_up(mh_in, 4)
         start_all(Z, send_mz)
 
     def pause_z():
         wait_all(Z, send_mz)
-        total = mh_z[0]
-        for s in range(1, Z):
-            total = total + mh_z[s]
-        mh_all[keep, :] = total
-        swap_m.start()
+        mh_all[my_tile] = add_up(mh_z, Z)
+        start_all(4, send_ma)
 
     swap_h.wait()
-    invert(hmat, left, right, {3: pause_core, 6: pause_bins, 11: pause_z})
-    swap_m.wait()
+    invert(hmat, left, right, {4: pause_quad, 9: pause_z})
+    wait_all(4, send_ma)
+    wait_all(Q, send_gcm)
+    swap_gc = remote(gcm.at[my_half], gcm.at[my_half], take(1), other_core)
 
     hf = jnp.dot(
         mh_all[...], hmat[...], precision=HIGHEST, preferred_element_type=f32
     )
-    my_hours = pl.ds(pl.multiple_of(h * hours, 8), hours)
+    my_hours = at(h, hours)
     hfall[my_hours, :] = hf
+    hf_base = take(NH)
+    send_hf = lambda d: remote(
+        hfall.at[my_hours], hfall.at[my_hours], hf_base + d, hour_block(d)
+    )
+    start_all(NH, send_hf)
+    swap_gc.start()
     hft[...] = hf.T
-    hf_base = base
-    send_hf = lambda d: remote(
-        hfall.at[my_hours], hfall.at[my_hours], hf_base + d, along_hours(d)
-    )
-    base += NH
-    start_all(NH, send_hf)
     hf_ref[...] = hf
 
     chunk = 32
@@ -399,26 +482,23 @@
             acc = acc + con[i, rows : rows + chunk, :] * weights[:, i : i + 1]
         mpt[rows : rows + chunk, :] = acc
     mp[...] = mpt[...].T
-    mp_base = base
+    mp_base = take(Q)
 
     def send_mp(d):
         t = lax.rem(q + d, Q)
-        rows = pl.ds(pl.multiple_of(t * mrow, 8), mrow)
-        return remote(mp.at[rows], mp_in.at[d], mp_base + d, plane(d))
-
-    base += Q
+        return remote(mp.at[at(t, mrow)], mp_in.at[d], mp_base + d, plane(d))
+
     start_all(Q, send_mp)
 
     wait_all(NH, send_hf)
     swap_gc.wait()
     hmat[...] = gram(hfall[...]) * gcm[...]
-    mine = pl.ds(pl.multiple_of(n * mrow, 8), mrow)
-    swap_o = remote(owned.at[mine], owned.at[mine], base, other_bins)
-    base += 1
+    mine = at(n, mrow)
+    swap_o = remote(owned.at[mine], owned.at[mine], take(1), other_bins)
 
     def pause_points():
         wait_all(Q, send_mp)
-        total = mp[pl.ds(pl.multiple_of(q * mrow, 8), mrow), :]
+        total = mp[at(q, mrow), :]
         for s in range(1, Q):
             total = total + mp_in[s]
         owned[mine, :] = total
@@ -433,7 +513,7 @@
 
 def local(sizes, tensor, b_factor, c_factor):
     NP, NH, NB = sizes
-    Z, Q = NP // 2, NH * NB
+    Z, Q, NX = NP // 2, NH * NB, NH // 2
     tensor = jnp.swapaxes(tensor, 1, 2)
     hours, bins, points = tensor.shape
     width = c_factor.shape[1]
@@ -441,7 +521,8 @@
     prow = width // (2 * Q)
     mrow = points // Q
     hh = hours // 2
-    sems = NH + 1 + 1 + Q + Z + Q + 2 + 1 + 1 + Z + 1 + NH + Q + 1
+    YC = 8
+    sems = 2 * NX + YC + 1 + 2 * Z + 3 * Q + 2 * NH + 11
     vm = lambda *shape: pltpu.VMEM(shape, f32)
     any_spec = pl.BlockSpec(memory_space=pltpu.HBM)
     vmem_spec = pl.BlockSpec(memory_space=pltpu.VMEM)
@@ -459,20 +540,19 @@
             vm(bins, width),
             pltpu.VMEM((2 * width, bins), bf16),
             vm(points, width),
+            vm(NX * brow // 2, width),
             vm(width, points),
             vm(width, width),
+            vm(YC, prow, width),
+            vm(Z, prow, width),
             vm(width, width),
             vm(prow, width),
-            vm(prow, width),
-            vm(Z, prow, width),
             vm(width, width),
             vm(width, width),
             vm(width, 128),
             vm(hours, width),
-            vm(hh, width),
-            vm(hh, width),
-            vm(hh, width),
-            vm(Z, hh, width),
+            vm(4, hh, width // 2),
+            vm(Z, hh, width // 2),
             vm(hours, width),
             vm(width, hours),
             vm(hours * NH, width),

time: 59.3 us -> 62.1 us (1.047)
  Pallas kernels: 55.7 us -> 57.9 us
    pallas_call x1, Pallas kernels: 55.7 us -> 57.9 us  [local(): pl.pallas_call(functools.partial(kernel, sizes), out_shape=(jax.ShapeDtyp...]
where the time goes in v3:
time: 62.1 us; the launch traced here: 61.3 us
  Pallas kernels  57.9 us (93%)
  local copies, waits for them, and re-layouts  2.7 us (4%)
  between operations  0.64 us (1%)
    pallas_call x1, Pallas kernels, local(): pl.pallas_call(functools.partial(kernel, sizes), out_shape=(jax.ShapeDtyp...  57.9 us
    unnamed x2, local copies, waits for them, and re-layouts  2.7 us

profile of v3, /device:TPU:8, one launch (start us, length us, event | category | flops | bytes accessed | tf_op | source)
XLA Modules:
  0.0 61.3 jit_solution(12403901610581293022)
XLA Ops:
  0.6 57.9 %shard_map.50 = (f32[16,256]{1,0:T(8,128)}, f32[32,256]{1,0:T(8,128)}) custom-call(f32[16,648,256]{2,1,0:T(8,128)} %bitcast.1, f32[32,256]{1,0:T(8,128)} %b_hbm.1, f32[648,256]{1,0:T(8,128)} %c_hbm.1), custom_call_target="tpu_custom_call" | custom-call | tf_op jit(solution)/shard_map/pallas_call | solution.py:529
  58.6 1.3 %copy.7 = f32[16,256]{1,0:T(8,128)} copy(f32[16,256]{1,0:T(8,128)} %get-tuple-element.4) | data formatting | bytes 32768
  59.9 1.4 %copy.8 = f32[32,256]{1,0:T(8,128)} copy(f32[32,256]{1,0:T(8,128)} %get-tuple-element.5) | data formatting | bytes 65536

commit v4 on v3

--- a/solution.py
+++ b/solution.py
@@ -169,13 +169,14 @@
     mh,
     mh_in,
     mh_z,
-    mh_all,
+    mhall,
     hft,
     hfall,
     mpt,
     mp,
     mp_in,
     owned,
+    owned_in,
     left,
     right,
     lsem,
@@ -185,6 +186,7 @@
     NP, NH, NB = sizes
     Z, Q, NX = NP // 2, NH * NB, NH // 2
     YC = 8
+    COL = (3, 8)
     hours, _, points = t_hbm.shape
     width = c_hbm.shape[1]
     half = width // 2
@@ -332,7 +334,7 @@
     def contract_hours(first, last):
         lax.fori_loop(first * hours // 16, last * hours // 16, contract, 0)
 
-    contract_hours(0, 1)
+    contract_hours(0, COL[0])
 
     wait_all(NX, send_x)
     gb_part[...] = gram(bx[...])
@@ -348,15 +350,23 @@
     start_all(YC, send_col)
     gb_in[w] = gb_part[my_rows, :]
 
+    bx_base = take(NX)
+    b_other = pl.ds(pl.multiple_of(h * brow + (1 - n) * bhalf, 8), bhalf)
+    send_b2 = lambda d: remote(
+        bbuf.at[b_other], bbuf.at[b_other], bx_base + d, along_x(d)
+    )
+    b_base = take(NH)
+    send_b = lambda d: remote(bbuf.at[my_b], bbuf.at[my_b], b_base + d, hour_block(d))
+    start_all(NX, send_b2)
+    start_all(NH, send_b, NX)
+
     chi, clo = ct[:width, :], ct[width:, :]
     mul = functools.partial(dot, dims=((1,), (1,)))
     gc_part[...] = mul(chi, chi) + (mul(chi, clo) + mul(clo, chi))
-    bins_rows = pl.ds(
-        pl.multiple_of(half * core + prow * (h * NB + 1 - n), 8), prow
-    )
-    send_gc = remote(gc_part.at[bins_rows], gc_in, take(1), other_bins)
+    my_half = at(core, half)
+    send_gc = remote(gc_part.at[my_half], gc_in, take(1), other_bins)
     send_gc.start()
-    contract_hours(1, 3)
+    contract_hours(COL[0], COL[1])
 
     def add_up(ref, count):
         total = ref[0]
@@ -369,37 +379,7 @@
     z_base = take(Z)
     send_gbz = lambda d: remote(gb_z.at[z], gb_z.at[z], z_base + d, along_z(d))
     start_all(Z, send_gbz)
-    contract_hours(3, 7)
-
-    wait_all(Z, send_gbz)
-    send_gc.wait()
-    gcm[my_rows, :] = gc_part[my_rows, :] + gc_in[...]
-    hmat[my_rows, :] = add_up(gb_z, Z) * gcm[my_rows, :]
-    h_base = take(Q)
-    send_h = lambda d: remote(hmat.at[my_rows], hmat.at[my_rows], h_base + d, plane(d))
-    start_all(Q, send_h)
-
-    bx_base = take(NX)
-    b_other = pl.ds(pl.multiple_of(h * brow + (1 - n) * bhalf, 8), bhalf)
-    send_b2 = lambda d: remote(
-        bbuf.at[b_other], bbuf.at[b_other], bx_base + d, along_x(d)
-    )
-    b_base = take(NH)
-    send_b = lambda d: remote(bbuf.at[my_b], bbuf.at[my_b], b_base + d, hour_block(d))
-    start_all(NX, send_b2)
-    start_all(NH, send_b, NX)
-    contract_hours(7, 13)
-
-    wait_all(Q, send_h)
-    my_half = at(core, half)
-    swap_h = remote(hmat.at[my_half], hmat.at[my_half], take(1), other_core)
-    swap_h.start()
-    gc_base = take(Q)
-    send_gcm = lambda d: remote(
-        gcm.at[my_rows], gcm.at[my_rows], gc_base + d, plane(d)
-    )
-    start_all(Q, send_gcm)
-    contract_hours(13, 16)
+    contract_hours(COL[1], 16)
 
     wait_all(NX, send_b2)
     wait_all(NH, send_b, NX)
@@ -439,38 +419,56 @@
     mh_in[g] = mh[my_tile]
     mz_base = take(Z)
     send_mz = lambda d: remote(mh_z.at[z], mh_z.at[z], mz_base + d, along_z(d))
+    my_hours = at(h, hours)
     ma_base = take(4)
+    my_part = (
+        pl.ds(pl.multiple_of(h * hours + core * hh, 8), hh),
+        pl.ds(pl.multiple_of(n * half, 128), half),
+    )
     send_ma = lambda d: remote(
-        mh_all.at[my_tile], mh_all.at[my_tile], ma_base + d, quad(d)
-    )
-
-    def pause_quad():
-        wait_all(4, send_mq)
-        mh_z[z] = add_up(mh_in, 4)
-        start_all(Z, send_mz)
+        mhall.at[my_part], mhall.at[my_part], ma_base + d, quad(d)
+    )
+    mr_base = take(NH)
+    send_mr = lambda d: remote(
+        mhall.at[my_hours], mhall.at[my_hours], mr_base + d, hour_block(d)
+    )
+
+    wait_all(Z, send_gbz)
+    send_gc.wait()
+    gcm[my_half, :] = gc_part[my_half, :] + gc_in[...]
+    swap_gc = remote(gcm.at[my_half], gcm.at[my_half], take(1), other_core)
+    hmat[my_rows, :] = add_up(gb_z, Z) * gcm[my_rows, :]
+    h_base = take(Q)
+    send_h = lambda d: remote(hmat.at[my_rows], hmat.at[my_rows], h_base + d, plane(d))
+    start_all(Q, send_h)
+    swap_gc.start()
+
+    wait_all(4, send_mq)
+    mh_z[z] = add_up(mh_in, 4)
+    start_all(Z, send_mz)
+
+    wait_all(Q, send_h)
+    swap_h = remote(hmat.at[my_half], hmat.at[my_half], take(1), other_core)
+    swap_h.start()
 
     def pause_z():
         wait_all(Z, send_mz)
-        mh_all[my_tile] = add_up(mh_z, Z)
+        mhall[my_part] = add_up(mh_z, Z)
         start_all(4, send_ma)
 
+    def pause_quad():
+        wait_all(4, send_ma)
+        start_all(NH, send_mr)
+
     swap_h.wait()
-    invert(hmat, left, right, {4: pause_quad, 9: pause_z})
-    wait_all(4, send_ma)
-    wait_all(Q, send_gcm)
-    swap_gc = remote(gcm.at[my_half], gcm.at[my_half], take(1), other_core)
-
-    hf = jnp.dot(
-        mh_all[...], hmat[...], precision=HIGHEST, preferred_element_type=f32
-    )
-    my_hours = at(h, hours)
-    hfall[my_hours, :] = hf
-    hf_base = take(NH)
-    send_hf = lambda d: remote(
-        hfall.at[my_hours], hfall.at[my_hours], hf_base + d, hour_block(d)
-    )
-    start_all(NH, send_hf)
-    swap_gc.start()
+    invert(hmat, left, right, {3: pause_z, 9: pause_quad})
+    wait_all(NH, send_mr)
+    swap_gc.wait()
+
+    hfall[...] = jnp.dot(
+        mhall[...], hmat[...], precision=HIGHEST, preferred_element_type=f32
+    )
+    hf = hfall[my_hours, :]
     hft[...] = hf.T
     hf_ref[...] = hf
 
@@ -482,32 +480,32 @@
             acc = acc + con[i, rows : rows + chunk, :] * weights[:, i : i + 1]
         mpt[rows : rows + chunk, :] = acc
     mp[...] = mpt[...].T
-    mp_base = take(Q)
+    mp_base = take(NH)
 
     def send_mp(d):
-        t = lax.rem(q + d, Q)
-        return remote(mp.at[at(t, mrow)], mp_in.at[d], mp_base + d, plane(d))
-
-    start_all(Q, send_mp)
-
-    wait_all(NH, send_hf)
-    swap_gc.wait()
+        flip = d // NX
+        h2 = lax.rem(y_hi + flip, 2) * NX + lax.rem(x + d, NX)
+        return remote(mp.at[at(h2, brow)], mp_in.at[d], mp_base + d, hour_block(d))
+
+    start_all(NH, send_mp)
     hmat[...] = gram(hfall[...]) * gcm[...]
-    mine = at(n, mrow)
-    swap_o = remote(owned.at[mine], owned.at[mine], take(1), other_bins)
+    swap_o = remote(owned, owned_in, take(1), other_bins)
 
     def pause_points():
-        wait_all(Q, send_mp)
-        total = mp[at(q, mrow), :]
-        for s in range(1, Q):
+        wait_all(NH, send_mp)
+        total = mp[my_b, :]
+        for s in range(1, NH):
             total = total + mp_in[s]
-        owned[mine, :] = total
+        owned[...] = total
         swap_o.start()
 
-    invert(hmat, left, right, {8: pause_points})
+    invert(hmat, left, right, {13: pause_points})
     swap_o.wait()
     pf_ref[...] = jnp.dot(
-        owned[...], hmat[...], precision=HIGHEST, preferred_element_type=f32
+        owned[...] + owned_in[...],
+        hmat[...],
+        precision=HIGHEST,
+        preferred_element_type=f32,
     )
 
 
@@ -546,19 +544,20 @@
             vm(YC, prow, width),
             vm(Z, prow, width),
             vm(width, width),
-            vm(prow, width),
+            vm(width // 2, width),
             vm(width, width),
             vm(width, width),
             vm(width, 128),
             vm(hours, width),
             vm(4, hh, width // 2),
             vm(Z, hh, width // 2),
-            vm(hours, width),
+            vm(hours * NH, width),
             vm(width, hours),
             vm(hours * NH, width),
             vm(width, points),
             vm(points, width),
-            vm(Q, mrow, width),
+            vm(NH, brow, width),
+            vm(brow, width),
             vm(brow, width),
             pltpu.VMEM((6 * STEP, width), bf16),
             pltpu.VMEM((6 * STEP, width), bf16),

time: 62.1 us -> 55.8 us (0.90); the launches traced: 61.3 us -> 55.6 us
  Pallas kernels: 57.9 us -> 52.3 us
    pallas_call x1, Pallas kernels: 57.9 us -> 52.3 us  [local(): pl.pallas_call(functools.partial(kernel, sizes), out_shape=(jax.ShapeDtyp...]
where the time goes in v4:
time: 55.8 us; the launch traced here: 55.6 us
  Pallas kernels  52.3 us (94%)
  local copies, waits for them, and re-layouts  2.7 us (5%)
  between operations  0.64 us (1%)
    pallas_call x1, Pallas kernels, local(): pl.pallas_call(functools.partial(kernel, sizes), out_shape=(jax.ShapeDtyp...  52.3 us
    unnamed x2, local copies, waits for them, and re-layouts  2.7 us

profile of v4, /device:TPU:8, one launch (start us, length us, event | category | flops | bytes accessed | tf_op | source)
XLA Modules:
  0.0 55.6 jit_solution(3302579648242013829)
XLA Ops:
  0.6 52.3 %shard_map.50 = (f32[16,256]{1,0:T(8,128)}, f32[32,256]{1,0:T(8,128)}) custom-call(f32[16,648,256]{2,1,0:T(8,128)} %bitcast.1, f32[32,256]{1,0:T(8,128)} %b_hbm.1, f32[648,256]{1,0:T(8,128)} %c_hbm.1), custom_call_target="tpu_custom_call" | custom-call | tf_op jit(solution)/shard_map/pallas_call | solution.py:527
  52.9 1.3 %copy.7 = f32[16,256]{1,0:T(8,128)} copy(f32[16,256]{1,0:T(8,128)} %get-tuple-element.4) | data formatting | bytes 32768
  54.3 1.4 %copy.8 = f32[32,256]{1,0:T(8,128)} copy(f32[32,256]{1,0:T(8,128)} %get-tuple-element.5) | data formatting | bytes 65536

commit v5 on v4

--- a/solution.py
+++ b/solution.py
@@ -26,8 +26,8 @@
 def gram(x):
     hi = x.astype(bf16).astype(f32)
     lo = x - hi
-    left = jnp.concatenate([hi, hi, lo, lo], axis=0).astype(bf16)
-    right = jnp.concatenate([hi, lo, hi, lo], axis=0).astype(bf16)
+    left = jnp.concatenate([hi, hi, lo], axis=0).astype(bf16)
+    right = jnp.concatenate([hi, lo, hi], axis=0).astype(bf16)
     return dot(left, right, ((0,), (0,)))
 
 
@@ -156,7 +156,6 @@
     cbuf,
     ct,
     bbuf,
-    bx,
     bt,
     gb_part,
     gb_in,
@@ -185,29 +184,21 @@
 ):
     NP, NH, NB = sizes
     Z, Q, NX = NP // 2, NH * NB, NH // 2
-    YC = 8
-    COL = (3, 8)
     hours, _, points = t_hbm.shape
     width = c_hbm.shape[1]
     half = width // 2
     prow = half // Q
     brow = b_hbm.shape[0]
-    bhalf = brow // 2
-    mrow = points // Q
     hh = hours // 2
     p, h, n = lax.axis_index("pts"), lax.axis_index("hrs"), lax.axis_index("bins")
     z, core = p // 2, lax.rem(p, 2)
     y_hi, x = h // NX, lax.rem(h, NX)
     q = h * NB + n
-    w = (2 * y_hi + n) * 2 + core
     g = 2 * core + n
 
     def plane(d):
         t = lax.rem(q + d, Q)
         return (p, t // NB, lax.rem(t, NB))
-
-    def along_x(d):
-        return (p, y_hi * NX + lax.rem(x + d, NX), n)
 
     def hour_block(d):
         flip = d // NX
@@ -219,14 +210,6 @@
 
     def along_z(d):
         return (lax.rem(z + d, Z) * 2 + core, h, n)
-
-    def split_w(d):
-        t = lax.rem(w + d, YC)
-        return t // 4, lax.rem(t // 2, 2), lax.rem(t, 2)
-
-    def column(d):
-        y2, n2, core2 = split_w(d)
-        return (z * 2 + core2, y2 * NX + x, n2)
 
     def quad(d):
         t = lax.rem(g + d, 4)
@@ -298,67 +281,33 @@
     lax.fori_loop(1, Q, greet(plane), 0)
     lax.fori_loop(1, Z, greet(along_z), 0)
 
-    def greet_column(i, _):
-        pl.semaphore_signal(
-            barrier,
-            inc=1,
-            device_id=(z * 2 + 1 - core, (i // 2) * NX + x, lax.rem(i, 2)),
-            device_id_type=MESH,
-        )
-        return 0
-
-    lax.fori_loop(0, YC // 2, greet_column, 0)
-    pl.semaphore_wait(barrier, Q - 1 + Z - 1 + YC // 2)
+    for device in (other_core, (p + 1 - 2 * core, h, 1 - n)):
+        pl.semaphore_signal(barrier, inc=1, device_id=device, device_id_type=MESH)
+    pl.semaphore_wait(barrier, Q - 1 + Z - 1 + 2)
 
     load_b.wait()
-    bx[at(x, bhalf), :] = bbuf[pl.ds(pl.multiple_of(h * brow + n * bhalf, 8), bhalf), :]
-    x_base = take(NX)
-    send_x = lambda d: remote(
-        bx.at[at(x, bhalf)], bx.at[at(x, bhalf)], x_base + d, along_x(d)
-    )
-    start_all(NX, send_x)
+    b_base = take(NH)
+    send_b = lambda d: remote(bbuf.at[my_b], bbuf.at[my_b], b_base + d, hour_block(d))
+    start_all(NH, send_b)
 
     load_c.wait()
     chi, clo = halves(cbuf[...].T)
     ct[:width, :] = chi
     ct[width:, :] = clo
 
+    group = 4
+
     def contract(i, _):
-        load_t(i).wait()
-        thi, tlo = halves(tbuf[i])
-        chi, clo = ct[:width, :], ct[width:, :]
-        mul = functools.partial(dot, dims=((1,), (0,)))
-        con[i] = mul(chi, thi) + (mul(clo, thi) + mul(chi, tlo))
+        for k in range(group):
+            hour = i * group + k
+            load_t(hour).wait()
+            thi, tlo = halves(tbuf[hour])
+            chi, clo = ct[:width, :], ct[width:, :]
+            mul = functools.partial(dot, dims=((1,), (0,)))
+            con[hour] = mul(chi, thi) + (mul(clo, thi) + mul(chi, tlo))
         return 0
 
-    def contract_hours(first, last):
-        lax.fori_loop(first * hours // 16, last * hours // 16, contract, 0)
-
-    contract_hours(0, COL[0])
-
-    wait_all(NX, send_x)
-    gb_part[...] = gram(bx[...])
-    my_rows = pl.ds(pl.multiple_of(half * core + prow * q, 8), prow)
-    col_base = take(YC)
-
-    def send_col(d):
-        y2, n2, core2 = split_w(d)
-        q2 = (y2 * NX + x) * NB + n2
-        rows = pl.ds(pl.multiple_of(half * core2 + prow * q2, 8), prow)
-        return remote(gb_part.at[rows], gb_in.at[w], col_base + d, column(d))
-
-    start_all(YC, send_col)
-    gb_in[w] = gb_part[my_rows, :]
-
-    bx_base = take(NX)
-    b_other = pl.ds(pl.multiple_of(h * brow + (1 - n) * bhalf, 8), bhalf)
-    send_b2 = lambda d: remote(
-        bbuf.at[b_other], bbuf.at[b_other], bx_base + d, along_x(d)
-    )
-    b_base = take(NH)
-    send_b = lambda d: remote(bbuf.at[my_b], bbuf.at[my_b], b_base + d, hour_block(d))
-    start_all(NX, send_b2)
-    start_all(NH, send_b, NX)
+    lax.fori_loop(0, hours // group, contract, 0)
 
     chi, clo = ct[:width, :], ct[width:, :]
     mul = functools.partial(dot, dims=((1,), (1,)))
@@ -366,7 +315,6 @@
     my_half = at(core, half)
     send_gc = remote(gc_part.at[my_half], gc_in, take(1), other_bins)
     send_gc.start()
-    contract_hours(COL[0], COL[1])
 
     def add_up(ref, count):
         total = ref[0]
@@ -374,33 +322,31 @@
             total = total + ref[s]
         return total
 
-    wait_all(YC, send_col)
-    gb_z[z] = add_up(gb_in, YC)
+    wait_all(NH, send_b)
+    gb_part[...] = gram(bbuf[...])
+    my_rows = pl.ds(pl.multiple_of(half * core + prow * q, 8), prow)
+    core_rows = pl.ds(pl.multiple_of(half * (1 - core) + prow * q, 8), prow)
+    send_gb = remote(gb_part.at[core_rows], gb_in, take(1), other_core)
+    send_gb.start()
+    bt[...] = bbuf[...].T
+    send_gb.wait()
+    gb_z[z] = gb_part[my_rows, :] + gb_in[...]
     z_base = take(Z)
     send_gbz = lambda d: remote(gb_z.at[z], gb_z.at[z], z_base + d, along_z(d))
     start_all(Z, send_gbz)
-    contract_hours(COL[1], 16)
-
-    wait_all(NX, send_b2)
-    wait_all(NH, send_b, NX)
-
-    def own_rows(d, _):
-        rows = pl.ds(
-            pl.multiple_of((y_hi * NX + d) * brow + n * bhalf, 8), bhalf
-        )
-        bbuf[rows, :] = bx[at(d, bhalf), :]
+
+    lane = lax.broadcasted_iota(jnp.int32, mht.shape, 1)
+
+    def partial_hours(i, _):
+        out = mht[...]
+        for k in range(group):
+            hour = i * group + k
+            total = jnp.sum(con[hour] * bt[...], axis=1, keepdims=True)
+            out = jnp.where(lane == hour, total, out)
+        mht[...] = out
         return 0
 
-    lax.fori_loop(0, NX, own_rows, 0)
-    bt[...] = bbuf[...].T
-    lane = lax.broadcasted_iota(jnp.int32, mht.shape, 1)
-
-    def partial_hours(i, _):
-        total = jnp.sum(con[i] * bt[...], axis=1, keepdims=True)
-        mht[...] = jnp.where(lane == i, total, mht[...])
-        return 0
-
-    lax.fori_loop(0, hours, partial_hours, 0)
+    lax.fori_loop(0, hours // group, partial_hours, 0)
     mh[...] = mht[...].T[:hours, :]
 
     def tile(c2, n2):
@@ -433,6 +379,10 @@
         mhall.at[my_hours], mhall.at[my_hours], mr_base + d, hour_block(d)
     )
 
+    wait_all(4, send_mq)
+    mh_z[z] = add_up(mh_in, 4)
+    start_all(Z, send_mz)
+
     wait_all(Z, send_gbz)
     send_gc.wait()
     gcm[my_half, :] = gc_part[my_half, :] + gc_in[...]
@@ -443,25 +393,17 @@
     start_all(Q, send_h)
     swap_gc.start()
 
-    wait_all(4, send_mq)
-    mh_z[z] = add_up(mh_in, 4)
-    start_all(Z, send_mz)
+    wait_all(Z, send_mz)
+    mhall[my_part] = add_up(mh_z, Z)
+    start_all(4, send_ma)
 
     wait_all(Q, send_h)
     swap_h = remote(hmat.at[my_half], hmat.at[my_half], take(1), other_core)
     swap_h.start()
-
-    def pause_z():
-        wait_all(Z, send_mz)
-        mhall[my_part] = add_up(mh_z, Z)
-        start_all(4, send_ma)
-
-    def pause_quad():
-        wait_all(4, send_ma)
-        start_all(NH, send_mr)
-
+    wait_all(4, send_ma)
+    start_all(NH, send_mr)
     swap_h.wait()
-    invert(hmat, left, right, {3: pause_z, 9: pause_quad})
+    invert(hmat, left, right, {})
     wait_all(NH, send_mr)
     swap_gc.wait()
 
@@ -511,16 +453,14 @@
 
 def local(sizes, tensor, b_factor, c_factor):
     NP, NH, NB = sizes
-    Z, Q, NX = NP // 2, NH * NB, NH // 2
+    Z, Q = NP // 2, NH * NB
     tensor = jnp.swapaxes(tensor, 1, 2)
     hours, bins, points = tensor.shape
     width = c_factor.shape[1]
     brow = b_factor.shape[0]
     prow = width // (2 * Q)
-    mrow = points // Q
     hh = hours // 2
-    YC = 8
-    sems = 2 * NX + YC + 1 + 2 * Z + 3 * Q + 2 * NH + 11
+    sems = 3 * Z + Q + 3 * NH + 8 + 6
     vm = lambda *shape: pltpu.VMEM(shape, f32)
     any_spec = pl.BlockSpec(memory_space=pltpu.HBM)
     vmem_spec = pl.BlockSpec(memory_space=pltpu.VMEM)
@@ -538,10 +478,9 @@
             vm(bins, width),
             pltpu.VMEM((2 * width, bins), bf16),
             vm(points, width),
-            vm(NX * brow // 2, width),
             vm(width, points),
             vm(width, width),
-            vm(YC, prow, width),
+            vm(prow, width),
             vm(Z, prow, width),
             vm(width, width),
             vm(width // 2, width),

time: 55.8 us -> 59.2 us (1.061)
  Pallas kernels: 52.3 us -> 55.7 us
    pallas_call x1, Pallas kernels: 52.3 us -> 55.7 us  [local(): pl.pallas_call(functools.partial(kernel, sizes), out_shape=(jax.ShapeDtyp...]
where the time goes in v5:
time: 59.2 us; the launch traced here: 59 us
  Pallas kernels  55.7 us (94%)
  local copies, waits for them, and re-layouts  2.7 us (5%)
  between operations  0.64 us (1%)
    pallas_call x1, Pallas kernels, local(): pl.pallas_call(functools.partial(kernel, sizes), out_shape=(jax.ShapeDtyp...  55.7 us
    unnamed x2, local copies, waits for them, and re-layouts  2.7 us

profile of v5, /device:TPU:8, one launch (start us, length us, event | category | flops | bytes accessed | tf_op | source)
XLA Modules:
  0.0 59.0 jit_solution(3987072995831131339)
XLA Ops:
  0.6 55.7 %shard_map.50 = (f32[16,256]{1,0:T(8,128)}, f32[32,256]{1,0:T(8,128)}) custom-call(f32[16,648,256]{2,1,0:T(8,128)} %bitcast.1, f32[32,256]{1,0:T(8,128)} %b_hbm.1, f32[648,256]{1,0:T(8,128)} %c_hbm.1), custom_call_target="tpu_custom_call" | custom-call | tf_op jit(solution)/shard_map/pallas_call | solution.py:467
  56.3 1.3 %copy.7 = f32[16,256]{1,0:T(8,128)} copy(f32[16,256]{1,0:T(8,128)} %get-tuple-element.4) | data formatting | bytes 32768
  57.6 1.4 %copy.8 = f32[32,256]{1,0:T(8,128)} copy(f32[32,256]{1,0:T(8,128)} %get-tuple-element.5) | data formatting | bytes 65536

commit v6 on v5

--- a/solution.py
+++ b/solution.py
@@ -299,8 +299,9 @@
 
     def contract(i, _):
         for k in range(group):
+            load_t(i * group + k).wait()
+        for k in range(group):
             hour = i * group + k
-            load_t(hour).wait()
             thi, tlo = halves(tbuf[hour])
             chi, clo = ct[:width, :], ct[width:, :]
             mul = functools.partial(dot, dims=((1,), (0,)))
@@ -449,6 +450,17 @@
         precision=HIGHEST,
         preferred_element_type=f32,
     )
+
+
+def write_out(hf_in, pf_in, hf_out, pf_out, sem):
+    copies = [
+        pltpu.make_async_copy(hf_in, hf_out, sem.at[0]),
+        pltpu.make_async_copy(pf_in, pf_out, sem.at[1]),
+    ]
+    for copy in copies:
+        copy.start()
+    for copy in copies:
+        copy.wait()
 
 
 def local(sizes, tensor, b_factor, c_factor):
@@ -464,12 +476,13 @@
     vm = lambda *shape: pltpu.VMEM(shape, f32)
     any_spec = pl.BlockSpec(memory_space=pltpu.HBM)
     vmem_spec = pl.BlockSpec(memory_space=pltpu.VMEM)
-    return pl.pallas_call(
+    out_shape = (
+        jax.ShapeDtypeStruct((hours, width), f32),
+        jax.ShapeDtypeStruct((brow, width), f32),
+    )
+    results = pl.pallas_call(
         functools.partial(kernel, sizes),
-        out_shape=(
-            jax.ShapeDtypeStruct((hours, width), f32),
-            jax.ShapeDtypeStruct((brow, width), f32),
-        ),
+        out_shape=out_shape,
         in_specs=[any_spec] * 3,
         out_specs=(vmem_spec, vmem_spec),
         scratch_shapes=[
@@ -510,6 +523,14 @@
             vmem_limit_bytes=56 * 1024 * 1024,
         ),
     )(tensor, b_factor, c_factor)
+    outer = pl.BlockSpec(memory_space=pl.ANY)
+    return pl.pallas_call(
+        write_out,
+        out_shape=out_shape,
+        in_specs=[outer] * 2,
+        out_specs=(outer, outer),
+        scratch_shapes=[pltpu.SemaphoreType.DMA((2,))],
+    )(*results)
 
 
 def solution(mesh):

time: 59.2 us -> 52.6 us (0.89)
  Pallas kernels: 55.7 us -> 51.8 us
  local copies, waits for them, and re-layouts: 2.7 us -> 0 us
    pallas_call x1 -> x2, Pallas kernels: 55.7 us -> 51.8 us  [the longest x1 49.2 us: local(): pl.pallas_call(functools.partial(kernel, sizes), out_shape=out_shape, in_...]
    unnamed x2 -> x0, local copies, waits for them, and re-layouts: 2.7 us -> none
where the time goes in v6:
time: 52.6 us; the launch traced here: 52.5 us
  Pallas kernels  51.8 us (98%)
  between operations  0.64 us (1%)
    pallas_call x1, Pallas kernels, local(): pl.pallas_call(functools.partial(kernel, sizes), out_shape=out_shape, in_...  49.2 us
    pallas_call x1, Pallas kernels, local(): pl.pallas_call(write_out, out_shape=out_shape, in_specs=[outer] * 2, out_...  2.61 us

profile of v6, /device:TPU:8, one launch (start us, length us, event | category | flops | bytes accessed | tf_op | source)
XLA Modules:
  0.0 52.5 jit_solution(17509942895453907487)
XLA Ops:
  0.6 49.2 %shard_map.50 = (f32[16,256]{1,0:T(8,128)}, f32[32,256]{1,0:T(8,128)}) custom-call(f32[16,648,256]{2,1,0:T(8,128)} %bitcast.1, f32[32,256]{1,0:T(8,128)} %b_hbm.1, f32[648,256]{1,0:T(8,128)} %c_hbm.1), custom_call_target="tpu_custom_call" | custom-call | tf_op jit(solution)/shard_map/pallas_call | solution.py:483
  49.9 2.6 %shard_map.51 = (f32[16,256]{1,0:T(8,128)}, f32[32,256]{1,0:T(8,128)}) custom-call(f32[16,256]{1,0:T(8,128)} %get-tuple-element.4.hf_in, f32[32,256]{1,0:T(8,128)} %get-tuple-element.5.pf_in), custom_call_target="tpu_custom_call" | custom-call | tf_op jit(solution)/shard_map/pallas_call | solution.py:527

commit v7 on v5

--- a/solution.py
+++ b/solution.py
@@ -134,10 +134,10 @@
     carry = (panel, done)
     first = 1
     for stop in sorted(pauses):
-        carry = lax.fori_loop(first, stop, body, carry)
+        carry = lax.fori_loop(first, stop, body, carry, unroll=2)
         pauses[stop]()
         first = stop
-    panel, before = lax.fori_loop(first, steps - 1, body, carry)
+    panel, before = lax.fori_loop(first, steps - 1, body, carry, unroll=2)
     late_update(a, left, right, at(steps - 2), before)
     done, column = pivot(panel, at(steps - 1))
     factors(left, right, column, done)
@@ -299,8 +299,9 @@
 
     def contract(i, _):
         for k in range(group):
+            load_t(i * group + k).wait()
+        for k in range(group):
             hour = i * group + k
-            load_t(hour).wait()
             thi, tlo = halves(tbuf[hour])
             chi, clo = ct[:width, :], ct[width:, :]
             mul = functools.partial(dot, dims=((1,), (0,)))
@@ -404,13 +405,11 @@
     start_all(NH, send_mr)
     swap_h.wait()
     invert(hmat, left, right, {})
-    wait_all(NH, send_mr)
-    swap_gc.wait()
-
-    hfall[...] = jnp.dot(
-        mhall[...], hmat[...], precision=HIGHEST, preferred_element_type=f32
-    )
-    hf = hfall[my_hours, :]
+
+    hour_rows = functools.partial(
+        jnp.dot, precision=HIGHEST, preferred_element_type=f32
+    )
+    hf = hour_rows(mhall[my_hours, :], hmat[...])
     hft[...] = hf.T
     hf_ref[...] = hf
 
@@ -430,6 +429,10 @@
         return remote(mp.at[at(h2, brow)], mp_in.at[d], mp_base + d, hour_block(d))
 
     start_all(NH, send_mp)
+
+    wait_all(NH, send_mr)
+    swap_gc.wait()
+    hfall[...] = hour_rows(mhall[...], hmat[...])
     hmat[...] = gram(hfall[...]) * gcm[...]
     swap_o = remote(owned, owned_in, take(1), other_bins)
 
@@ -464,12 +467,13 @@
     vm = lambda *shape: pltpu.VMEM(shape, f32)
     any_spec = pl.BlockSpec(memory_space=pltpu.HBM)
     vmem_spec = pl.BlockSpec(memory_space=pltpu.VMEM)
+    out_shape = (
+        jax.ShapeDtypeStruct((hours, width), f32),
+        jax.ShapeDtypeStruct((brow, width), f32),
+    )
     return pl.pallas_call(
         functools.partial(kernel, sizes),
-        out_shape=(
-            jax.ShapeDtypeStruct((hours, width), f32),
-            jax.ShapeDtypeStruct((brow, width), f32),
-        ),
+        out_shape=out_shape,
         in_specs=[any_spec] * 3,
         out_specs=(vmem_spec, vmem_spec),
         scratch_shapes=[
@@ -507,7 +511,7 @@
         compiler_params=pltpu.CompilerParams(
             collective_id=0,
             has_side_effects=True,
-            vmem_limit_bytes=56 * 1024 * 1024,
+            vmem_limit_bytes=54784 * 1024,
         ),
     )(tensor, b_factor, c_factor)
 

time: 59.2 us -> 50.5 us (0.85)
  Pallas kernels: 55.7 us -> 47.7 us
  local copies, waits for them, and re-layouts: 2.7 us -> 1.97 us
    pallas_call x1, Pallas kernels: 55.7 us -> 47.7 us  [local(): pl.pallas_call(functools.partial(kernel, sizes), out_shape=out_shape, in_...]
    unnamed x2 -> x4, local copies, waits for them, and re-layouts: 2.7 us -> 1.97 us
where the time goes in v7:
time: 50.5 us; the launch traced here: 50.3 us
  Pallas kernels  47.7 us (94%)
  local copies, waits for them, and re-layouts  1.97 us (4%)
  between operations  0.65 us (1%)
    pallas_call x1, Pallas kernels, local(): pl.pallas_call(functools.partial(kernel, sizes), out_shape=out_shape, in_...  47.7 us
    unnamed x4, local copies, waits for them, and re-layouts  1.97 us

profile of v7, /device:TPU:8, one launch (start us, length us, event | category | flops | bytes accessed | tf_op | source)
XLA Modules:
  0.0 50.3 jit_solution(10900335446220336668)
XLA Ops:
  0.6 0.0 copy-start
  0.6 0.7 %copy-done = f32[32,256]{1,0:T(8,128)S(1)} copy-done((f32[32,256]{1,0:T(8,128)S(1)}, f32[32,256]{1,0:T(8,128)}, u32[]{:S(2)}) %copy-start) | copy-done | bytes 32792
  1.4 47.7 %shard_map.50 = (f32[16,256]{1,0:T(8,128)S(1)}, f32[32,256]{1,0:T(8,128)S(1)}) custom-call(f32[16,648,256]{2,1,0:T(8,128)} %bitcast.1, f32[32,256]{1,0:T(8,128)S(1)} %copy-done, f32[648,256]{1,0:T(8,128)} %c_hbm.1), custom_call_target="tpu_custom_call" | custom-call | tf_op jit(solution)/shard_map/pallas_call | solution.py:474
  49.1 0.6 %copy.7 = f32[16,256]{1,0:T(8,128)} copy(f32[16,256]{1,0:T(8,128)S(1)} %get-tuple-element.4) | data formatting | bytes 32768
  49.7 0.6 %copy.8 = f32[32,256]{1,0:T(8,128)} copy(f32[32,256]{1,0:T(8,128)S(1)} %get-tuple-element.5) | data formatting | bytes 65536
Async XLA Ops:
  0.6 0.8 %copy-start = (f32[32,256]{1,0:T(8,128)S(1)}, f32[32,256]{1,0:T(8,128)}, u32[]{:S(2)}) copy-start(f32[32,256]{1,0:T(8,128)} %b_hbm.1) | copy-start | bytes 98308

commit v8 on v7

--- a/solution.py
+++ b/solution.py
@@ -295,6 +295,13 @@
     ct[:width, :] = chi
     ct[width:, :] = clo
 
+    chi, clo = ct[:width, :], ct[width:, :]
+    mul = functools.partial(dot, dims=((1,), (1,)))
+    gc_part[...] = mul(chi, chi) + (mul(chi, clo) + mul(clo, chi))
+    my_half = at(core, half)
+    send_gc = remote(gc_part.at[my_half], gc_in, take(1), other_bins)
+    send_gc.start()
+
     group = 4
 
     def contract(i, _):
@@ -310,12 +317,6 @@
 
     lax.fori_loop(0, hours // group, contract, 0)
 
-    chi, clo = ct[:width, :], ct[width:, :]
-    mul = functools.partial(dot, dims=((1,), (1,)))
-    gc_part[...] = mul(chi, chi) + (mul(chi, clo) + mul(clo, chi))
-    my_half = at(core, half)
-    send_gc = remote(gc_part.at[my_half], gc_in, take(1), other_bins)
-    send_gc.start()
 
     def add_up(ref, count):
         total = ref[0]
@@ -413,22 +414,34 @@
     hft[...] = hf.T
     hf_ref[...] = hf
 
+    mp_base = take(2 * NH)
+
+    def send_mp(s):
+        lanes = slice(s * half, (s + 1) * half)
+
+        def make(d):
+            flip = d // NX
+            h2 = lax.rem(y_hi + flip, 2) * NX + lax.rem(x + d, NX)
+            return remote(
+                mp.at[at(h2, brow), lanes],
+                mp_in.at[d, :, lanes],
+                mp_base + s * NH + d,
+                hour_block(d),
+            )
+
+        return make
+
     chunk = 32
-    for rows in range(0, width, chunk):
-        weights = hft[rows : rows + chunk, :]
-        acc = con[0, rows : rows + chunk, :] * weights[:, 0:1]
-        for i in range(1, hours):
-            acc = acc + con[i, rows : rows + chunk, :] * weights[:, i : i + 1]
-        mpt[rows : rows + chunk, :] = acc
-    mp[...] = mpt[...].T
-    mp_base = take(NH)
-
-    def send_mp(d):
-        flip = d // NX
-        h2 = lax.rem(y_hi + flip, 2) * NX + lax.rem(x + d, NX)
-        return remote(mp.at[at(h2, brow)], mp_in.at[d], mp_base + d, hour_block(d))
-
-    start_all(NH, send_mp)
+    for s in range(2):
+        for rows in range(s * half, (s + 1) * half, chunk):
+            weights = hft[rows : rows + chunk, :]
+            acc = con[0, rows : rows + chunk, :] * weights[:, 0:1]
+            for i in range(1, hours):
+                acc = acc + con[i, rows : rows + chunk, :] * weights[:, i : i + 1]
+            mpt[rows : rows + chunk, :] = acc
+        lanes = slice(s * half, (s + 1) * half)
+        mp[:, lanes] = mpt[lanes, :].T
+        start_all(NH, send_mp(s))
 
     wait_all(NH, send_mr)
     swap_gc.wait()
@@ -437,7 +450,8 @@
     swap_o = remote(owned, owned_in, take(1), other_bins)
 
     def pause_points():
-        wait_all(NH, send_mp)
+        wait_all(NH, send_mp(0))
+        wait_all(NH, send_mp(1))
         total = mp[my_b, :]
         for s in range(1, NH):
             total = total + mp_in[s]
@@ -463,7 +477,7 @@
     brow = b_factor.shape[0]
     prow = width // (2 * Q)
     hh = hours // 2
-    sems = 3 * Z + Q + 3 * NH + 8 + 6
+    sems = 2 * Z + Q + 4 * NH + 8 + 6
     vm = lambda *shape: pltpu.VMEM(shape, f32)
     any_spec = pl.BlockSpec(memory_space=pltpu.HBM)
     vmem_spec = pl.BlockSpec(memory_space=pltpu.VMEM)
@@ -511,7 +525,7 @@
         compiler_params=pltpu.CompilerParams(
             collective_id=0,
             has_side_effects=True,
-            vmem_limit_bytes=54784 * 1024,
+            vmem_limit_bytes=55160 * 1024,
         ),
     )(tensor, b_factor, c_factor)
 

time: 50.5 us -> 48.8 us (0.966)
  Pallas kernels: 47.7 us -> 46.8 us
  local copies, waits for them, and re-layouts: 1.97 us -> 1.22 us
    pallas_call x1, Pallas kernels: 47.7 us -> 46.8 us  [local(): pl.pallas_call(functools.partial(kernel, sizes), out_shape=out_shape, in_...]
    unnamed x4 -> x2, local copies, waits for them, and re-layouts: 1.97 us -> 1.22 us
where the time goes in v8:
time: 48.8 us; the launch traced here: 48.7 us
  Pallas kernels  46.8 us (96%)
  local copies, waits for them, and re-layouts  1.22 us (2%)
  between operations  0.64 us (1%)
    pallas_call x1, Pallas kernels, local(): pl.pallas_call(functools.partial(kernel, sizes), out_shape=out_shape, in_...  46.8 us
    unnamed x2, local copies, waits for them, and re-layouts  1.22 us

profile of v8, /device:TPU:8, one launch (start us, length us, event | category | flops | bytes accessed | tf_op | source)
XLA Modules:
  0.0 48.7 jit_solution(13895095066882161105)
XLA Ops:
  0.6 46.8 %shard_map.50 = (f32[16,256]{1,0:T(8,128)S(1)}, f32[32,256]{1,0:T(8,128)S(1)}) custom-call(f32[16,648,256]{2,1,0:T(8,128)} %bitcast.1, f32[32,256]{1,0:T(8,128)} %b_hbm.1, f32[648,256]{1,0:T(8,128)} %c_hbm.1), custom_call_target="tpu_custom_call" | custom-call | tf_op jit(solution)/shard_map/pallas_call | solution.py:488
  47.5 0.6 %copy.7 = f32[16,256]{1,0:T(8,128)} copy(f32[16,256]{1,0:T(8,128)S(1)} %get-tuple-element.4) | data formatting | bytes 32768
  48.1 0.6 %copy.8 = f32[32,256]{1,0:T(8,128)} copy(f32[32,256]{1,0:T(8,128)S(1)} %get-tuple-element.5) | data formatting | bytes 65536

commit v9 on v8

--- a/solution.py
+++ b/solution.py
@@ -113,7 +113,7 @@
     a[pl.ds(row, STEP), :] = done
 
 
-def invert(a, left, right, pauses):
+def invert(a, left, right, pauses, unroll):
     steps = a.shape[0] // STEP
 
     def at(k):
@@ -134,10 +134,10 @@
     carry = (panel, done)
     first = 1
     for stop in sorted(pauses):
-        carry = lax.fori_loop(first, stop, body, carry, unroll=2)
+        carry = lax.fori_loop(first, stop, body, carry, unroll=unroll)
         pauses[stop]()
         first = stop
-    panel, before = lax.fori_loop(first, steps - 1, body, carry, unroll=2)
+    panel, before = lax.fori_loop(first, steps - 1, body, carry, unroll=unroll)
     late_update(a, left, right, at(steps - 2), before)
     done, column = pivot(panel, at(steps - 1))
     factors(left, right, column, done)
@@ -256,7 +256,6 @@
     load_b = pltpu.make_async_copy(b_hbm, bbuf.at[my_b], lsem.at[hours])
     load_c = pltpu.make_async_copy(c_hbm, cbuf, lsem.at[hours + 1])
     load_b.start()
-    load_c.start()
 
     def load_t(i):
         return pltpu.make_async_copy(t_hbm.at[i], tbuf.at[i], lsem.at[i])
@@ -264,8 +263,6 @@
     def start_t(i, _):
         load_t(i).start()
         return 0
-
-    lax.fori_loop(0, hours, start_t, 0)
 
     barrier = pltpu.get_barrier_semaphore()
 
@@ -283,6 +280,8 @@
 
     for device in (other_core, (p + 1 - 2 * core, h, 1 - n)):
         pl.semaphore_signal(barrier, inc=1, device_id=device, device_id_type=MESH)
+    load_c.start()
+    lax.fori_loop(0, hours, start_t, 0)
     pl.semaphore_wait(barrier, Q - 1 + Z - 1 + 2)
 
     load_b.wait()
@@ -405,7 +404,7 @@
     wait_all(4, send_ma)
     start_all(NH, send_mr)
     swap_h.wait()
-    invert(hmat, left, right, {})
+    invert(hmat, left, right, {}, 7)
 
     hour_rows = functools.partial(
         jnp.dot, precision=HIGHEST, preferred_element_type=f32
@@ -447,19 +446,28 @@
     swap_gc.wait()
     hfall[...] = hour_rows(mhall[...], hmat[...])
     hmat[...] = gram(hfall[...]) * gcm[...]
-    swap_o = remote(owned, owned_in, take(1), other_bins)
-
-    def pause_points():
-        wait_all(NH, send_mp(0))
-        wait_all(NH, send_mp(1))
-        total = mp[my_b, :]
-        for s in range(1, NH):
-            total = total + mp_in[s]
-        owned[...] = total
-        swap_o.start()
-
-    invert(hmat, left, right, {13: pause_points})
-    swap_o.wait()
+    o_base = take(2)
+
+    def swap_o(s):
+        lanes = slice(s * half, (s + 1) * half)
+        return remote(owned.at[:, lanes], owned_in.at[:, lanes], o_base + s, other_bins)
+
+    def pause_points(s):
+        lanes = slice(s * half, (s + 1) * half)
+
+        def pause():
+            wait_all(NH, send_mp(s))
+            total = mp[my_b, lanes]
+            for d in range(1, NH):
+                total = total + mp_in[d, :, lanes]
+            owned[:, lanes] = total
+            swap_o(s).start()
+
+        return pause
+
+    invert(hmat, left, right, {9: pause_points(0), 13: pause_points(1)}, 2)
+    swap_o(0).wait()
+    swap_o(1).wait()
     pf_ref[...] = jnp.dot(
         owned[...] + owned_in[...],
         hmat[...],

time: 48.8 us -> 48.9 us (level)
  no operation moved by 1% of the time
where the time goes in v9:
time: 48.9 us; the launch traced here: 48.8 us
  Pallas kernels  47 us (96%)
  local copies, waits for them, and re-layouts  1.22 us (2%)
  between operations  0.64 us (1%)
    pallas_call x1, Pallas kernels, local(): pl.pallas_call(functools.partial(kernel, sizes), out_shape=out_shape, in_...  47 us
    unnamed x2, local copies, waits for them, and re-layouts  1.22 us

profile of v9, /device:TPU:8, one launch (start us, length us, event | category | flops | bytes accessed | tf_op | source)
XLA Modules:
  0.0 48.8 jit_solution(12636864142536750386)
XLA Ops:
  0.6 47.0 %shard_map.50 = (f32[16,256]{1,0:T(8,128)S(1)}, f32[32,256]{1,0:T(8,128)S(1)}) custom-call(f32[16,648,256]{2,1,0:T(8,128)} %bitcast.1, f32[32,256]{1,0:T(8,128)} %b_hbm.1, f32[648,256]{1,0:T(8,128)} %c_hbm.1), custom_call_target="tpu_custom_call" | custom-call | tf_op jit(solution)/shard_map/pallas_call | solution.py:496
  47.6 0.6 %copy.7 = f32[16,256]{1,0:T(8,128)} copy(f32[16,256]{1,0:T(8,128)S(1)} %get-tuple-element.4) | data formatting | bytes 32768
  48.2 0.6 %copy.8 = f32[32,256]{1,0:T(8,128)} copy(f32[32,256]{1,0:T(8,128)S(1)} %get-tuple-element.5) | data formatting | bytes 65536

commit v10 on v9

--- a/solution.py
+++ b/solution.py
@@ -235,6 +235,13 @@
 
         lax.fori_loop(first, count, body, 0)
 
+    def start_far_first(count, make, ring):
+        def distance(d):
+            return min(d % ring, ring - d % ring)
+
+        for d in sorted(range(1, count), key=distance, reverse=True):
+            make(d).start()
+
     def wait_all(count, make, first=1):
         def body(d, _):
             make(d).wait()
@@ -287,7 +294,7 @@
     load_b.wait()
     b_base = take(NH)
     send_b = lambda d: remote(bbuf.at[my_b], bbuf.at[my_b], b_base + d, hour_block(d))
-    start_all(NH, send_b)
+    start_far_first(NH, send_b, NX)
 
     load_c.wait()
     chi, clo = halves(cbuf[...].T)
@@ -334,7 +341,7 @@
     gb_z[z] = gb_part[my_rows, :] + gb_in[...]
     z_base = take(Z)
     send_gbz = lambda d: remote(gb_z.at[z], gb_z.at[z], z_base + d, along_z(d))
-    start_all(Z, send_gbz)
+    start_far_first(Z, send_gbz, Z)
 
     lane = lax.broadcasted_iota(jnp.int32, mht.shape, 1)
 
@@ -382,7 +389,7 @@
 
     wait_all(4, send_mq)
     mh_z[z] = add_up(mh_in, 4)
-    start_all(Z, send_mz)
+    start_far_first(Z, send_mz, Z)
 
     wait_all(Z, send_gbz)
     send_gc.wait()
@@ -402,7 +409,7 @@
     swap_h = remote(hmat.at[my_half], hmat.at[my_half], take(1), other_core)
     swap_h.start()
     wait_all(4, send_ma)
-    start_all(NH, send_mr)
+    start_far_first(NH, send_mr, NX)
     swap_h.wait()
     invert(hmat, left, right, {}, 7)
 
@@ -440,7 +447,7 @@
             mpt[rows : rows + chunk, :] = acc
         lanes = slice(s * half, (s + 1) * half)
         mp[:, lanes] = mpt[lanes, :].T
-        start_all(NH, send_mp(s))
+        start_far_first(NH, send_mp(s), NX)
 
     wait_all(NH, send_mr)
     swap_gc.wait()

time: 48.9 us -> 48.3 us (0.988)
  Pallas kernels: 47 us -> 46.4 us
    pallas_call x1, Pallas kernels: 47 us -> 46.4 us  [local(): pl.pallas_call(functools.partial(kernel, sizes), out_shape=out_shape, in_...]
where the time goes in v10:
time: 48.3 us
  Pallas kernels  46.4 us (96%)
  local copies, waits for them, and re-layouts  1.22 us (3%)
  between operations  0.64 us (1%)
    pallas_call x1, Pallas kernels, local(): pl.pallas_call(functools.partial(kernel, sizes), out_shape=out_shape, in_...  46.4 us
    unnamed x2, local copies, waits for them, and re-layouts  1.22 us

profile of v10, /device:TPU:8, one launch (start us, length us, event | category | flops | bytes accessed | tf_op | source)
XLA Modules:
  0.0 48.3 jit_solution(5622554054085398168)
XLA Ops:
  0.6 46.4 %shard_map.50 = (f32[16,256]{1,0:T(8,128)S(1)}, f32[32,256]{1,0:T(8,128)S(1)}) custom-call(f32[16,648,256]{2,1,0:T(8,128)} %bitcast.1, f32[32,256]{1,0:T(8,128)} %b_hbm.1, f32[648,256]{1,0:T(8,128)} %c_hbm.1), custom_call_target="tpu_custom_call" | custom-call | tf_op jit(solution)/shard_map/pallas_call | solution.py:503
  47.0 0.6 %copy.7 = f32[16,256]{1,0:T(8,128)} copy(f32[16,256]{1,0:T(8,128)S(1)} %get-tuple-element.4) | data formatting | bytes 32768
  47.6 0.6 %copy.8 = f32[32,256]{1,0:T(8,128)} copy(f32[32,256]{1,0:T(8,128)S(1)} %get-tuple-element.5) | data formatting | bytes 65536
